TPU v7x, 32 devices: a whole 2x2x4 slice. The times are simulated.
32 devices in a mesh: dp: 8 (over z, x), tensor: 4 (over y, core).
Axes of the slice: x: 2, y: 2, z: 4, core: 2. Of those that a mesh axis runs over, the one named last changes fastest.
Arguments:
- tokens: bfloat16 [16384, 1152], P(('dp', 'tensor')), may hold values from -6 to 6
- gain_one: float32 [1152], replicated, may hold values from 0.5 to 1.5
- shift_one: float32 [1152], replicated, may hold values from -2 to 2
- w_query: float32 [1152, 1152], P('dp', 'tensor'), may hold values from -0.25 to 0.25
- b_query: float32 [1152], replicated, may hold values from -2 to 2
- w_key: float32 [1152, 1152], P('dp', 'tensor'), may hold values from -0.25 to 0.25
- w_value: float32 [1152, 1152], P('dp', 'tensor'), may hold values from -0.1875 to 0.1875
- b_value: float32 [1152], replicated, may hold values from -2 to 2
- w_out: float32 [1152, 1152], P('tensor', 'dp'), may hold values from -0.75 to 0.75
- b_out: float32 [1152], replicated, may hold values from -2 to 2
- gain_two: float32 [1152], replicated, may hold values from 0.5 to 1.5
- shift_two: float32 [1152], replicated, may hold values from -2 to 2
- w_up: float32 [1152, 4304], P('dp', 'tensor'), may hold values from -0.1875 to 0.1875
- b_up: float32 [4304], replicated, may hold values from -2 to 2
- w_down: float32 [4304, 1152], P('tensor', 'dp'), may hold values from -0.09375 to 0.09375
- b_down: float32 [1152], replicated, may hold values from -2 to 2
- cotangent: bfloat16 [16384, 1152], P(('dp', 'tensor')), may hold values from -6 to 6
Outputs:
- output: bfloat16 [16384, 1152], P(('dp', 'tensor'))
- grad_tokens: bfloat16 [16384, 1152], P(('dp', 'tensor'))
- grad_gain_one: float32 [1152], replicated
- grad_shift_one: float32 [1152], replicated
- grad_w_query: float32 [1152, 1152], P('dp', 'tensor')
- grad_b_query: float32 [1152], replicated
- grad_w_key: float32 [1152, 1152], P('dp', 'tensor')
- grad_w_value: float32 [1152, 1152], P('dp', 'tensor')
- grad_b_value: float32 [1152], replicated
- grad_w_out: float32 [1152, 1152], P('tensor', 'dp')
- grad_b_out: float32 [1152], replicated
- grad_gain_two: float32 [1152], replicated
- grad_shift_two: float32 [1152], replicated
- grad_w_up: float32 [1152, 4304], P('dp', 'tensor')
- grad_b_up: float32 [4304], replicated
- grad_w_down: float32 [4304, 1152], P('tensor', 'dp')
- grad_b_down: float32 [1152], replicated
All inputs are finite; a program needn't handle non-finite values.
Results may differ from a plain program's by a relative error of at most 0.02.
Values may be sent and summed in bfloat16 or wider, within the bound.
No kernel may reach another device: no remote copies, remote signals or barrier semaphores. Data moves between devices by JAX's collectives and lax.ppermute only.
A program may use at most 192 MiB of HBM per device.

v0:
```python
import jax
import jax.numpy as jnp
from jax import lax
from jax.sharding import PartitionSpec as P

HD = 72
LEN = 1024


norm_eps = 1e-06


def layer_norm(values, norm_gain, norm_shift):
    centred = values - jnp.mean(values, axis=-1, keepdims=True)
    spread = jnp.mean(centred * centred, axis=-1, keepdims=True)
    return centred * lax.rsqrt(spread + norm_eps) * norm_gain + norm_shift


def gelu_tanh(values):
    return jax.nn.gelu(values, approximate=True)


def contract_rows(left, right):
    return lax.dot_general(
        left, right, (((0,), (0,)), ((), ())), preferred_element_type=jnp.float32
    )


def contract_cols(left, right):
    return lax.dot_general(
        left, right, (((1,), (1,)), ((), ())), preferred_element_type=jnp.float32
    )


def place_slice(vector_part, slot_index, full_length):
    blank = jnp.zeros((full_length,), jnp.float32)
    return lax.dynamic_update_slice_in_dim(blank, vector_part, slot_index * vector_part.shape[0], 0)


def attend_forward(parts_in):
    queries_img, keys_img, values_img = parts_in
    heads_dev = queries_img.shape[1]
    block_rows = min(512, LEN)
    query_blocks = queries_img.reshape(LEN // block_rows, block_rows, heads_dev, HD)
    scale_factor = HD ** (-0.5)

    def one_block(query_block):
        scores = (
            jnp.einsum("qhd,khd->hqk", query_block, keys_img, preferred_element_type=jnp.float32)
            * scale_factor
        )
        highest = jnp.max(scores, axis=-1, keepdims=True)
        exponent = jnp.exp(scores - highest)
        denominator = jnp.sum(exponent, axis=-1, keepdims=True)
        probs_low = (exponent / denominator).astype(jnp.bfloat16)
        mixed_block = jnp.einsum(
            "hqk,khd->qhd", probs_low, values_img, preferred_element_type=jnp.float32
        )
        return (mixed_block.astype(jnp.bfloat16), (highest + jnp.log(denominator))[:, :, 0])

    mixed_blocks, log_blocks = lax.map(one_block, query_blocks)
    return (mixed_blocks.reshape(LEN, heads_dev, HD), log_blocks)


def attend_backward(parts_in):
    queries_img, keys_img, values_img, grads_img, log_blocks = parts_in
    heads_dev = queries_img.shape[1]
    block_rows = min(512, LEN)
    query_blocks = queries_img.reshape(LEN // block_rows, block_rows, heads_dev, HD)
    grad_blocks = grads_img.reshape(LEN // block_rows, block_rows, heads_dev, HD)
    scale_factor = HD ** (-0.5)

    def one_block(carry, block_parts):
        key_sum, value_sum = carry
        query_block, grad_block, log_block = block_parts
        scores = (
            jnp.einsum("qhd,khd->hqk", query_block, keys_img, preferred_element_type=jnp.float32)
            * scale_factor
        )
        probs = jnp.exp(scores - log_block[:, :, None])
        probs_low = probs.astype(jnp.bfloat16)
        value_sum = value_sum + jnp.einsum(
            "hqk,qhd->khd", probs_low, grad_block, preferred_element_type=jnp.float32
        )
        prob_grad = jnp.einsum(
            "qhd,khd->hqk", grad_block, values_img, preferred_element_type=jnp.float32
        )
        centre = jnp.sum(probs * prob_grad, axis=-1, keepdims=True)
        score_grad = (probs * (prob_grad - centre)).astype(jnp.bfloat16)
        query_grad = (
            jnp.einsum("hqk,khd->qhd", score_grad, keys_img, preferred_element_type=jnp.float32)
            * scale_factor
        )
        key_sum = (
            key_sum
            + jnp.einsum(
                "hqk,qhd->khd", score_grad, query_block, preferred_element_type=jnp.float32
            )
            * scale_factor
        )
        return ((key_sum, value_sum), query_grad.astype(jnp.bfloat16))

    blank = jnp.zeros((LEN, heads_dev, HD), jnp.float32)
    (key_sum, value_sum), query_grads = lax.scan(
        one_block, (blank, blank), (query_blocks, grad_blocks, log_blocks)
    )
    return (
        query_grads.reshape(LEN, heads_dev, HD),
        key_sum.astype(jnp.bfloat16),
        value_sum.astype(jnp.bfloat16),
    )


def local(
    tokens,
    gain_one,
    shift_one,
    w_query,
    b_query,
    w_key,
    w_value,
    b_value,
    w_out,
    b_out,
    gain_two,
    shift_two,
    w_up,
    b_up,
    w_down,
    b_down,
    cotangent,
):
    tensor_rank = lax.axis_index("tensor")
    head_cols = w_query.shape[1]
    hidden_cols = w_up.shape[1]
    heads_dev = head_cols // HD
    query_full, key_full, value_full, out_full, up_full, down_full = (
        lax.all_gather(w_query.astype(jnp.bfloat16), "dp", axis=0, tiled=True),
        lax.all_gather(w_key.astype(jnp.bfloat16), "dp", axis=0, tiled=True),
        lax.all_gather(w_value.astype(jnp.bfloat16), "dp", axis=0, tiled=True),
        lax.all_gather(w_out.astype(jnp.bfloat16), "dp", axis=1, tiled=True),
        lax.all_gather(w_up.astype(jnp.bfloat16), "dp", axis=0, tiled=True),
        lax.all_gather(w_down.astype(jnp.bfloat16), "dp", axis=1, tiled=True),
    )
    query_bias = lax.dynamic_slice_in_dim(b_query, tensor_rank * head_cols, head_cols)
    value_bias = lax.dynamic_slice_in_dim(b_value, tensor_rank * head_cols, head_cols)
    inputs32 = tokens.astype(jnp.float32)
    normed_one = layer_norm(inputs32, gain_one, shift_one).astype(jnp.bfloat16)
    rows_one = lax.all_gather(normed_one, "tensor", axis=0, tiled=True)
    group_rows = rows_one.shape[0]
    images = group_rows // LEN
    queries_low = (
        jnp.dot(rows_one, query_full, preferred_element_type=jnp.float32) + query_bias
    ).astype(jnp.bfloat16)
    keys_low = jnp.dot(rows_one, key_full, preferred_element_type=jnp.float32).astype(jnp.bfloat16)
    values_low = (
        jnp.dot(rows_one, value_full, preferred_element_type=jnp.float32) + value_bias
    ).astype(jnp.bfloat16)

    def by_image(matrix):
        return matrix.reshape(images, LEN, heads_dev, HD)

    mixed_low, log_totals = lax.map(
        attend_forward, (by_image(queries_low), by_image(keys_low), by_image(values_low))
    )
    mixed_low = mixed_low.reshape(group_rows, head_cols)
    attn_sum = lax.psum_scatter(
        jnp.dot(mixed_low, out_full, preferred_element_type=jnp.float32).astype(jnp.bfloat16),
        "tensor",
        scatter_dimension=0,
        tiled=True,
    ).astype(jnp.float32)
    residual = inputs32 + attn_sum + b_out
    normed_two = layer_norm(residual, gain_two, shift_two).astype(jnp.bfloat16)
    rows_two = lax.all_gather(normed_two, "tensor", axis=0, tiled=True)
    up_bias = lax.dynamic_slice_in_dim(b_up, tensor_rank * hidden_cols, hidden_cols)
    pre_act = jnp.dot(rows_two, up_full, preferred_element_type=jnp.float32) + up_bias
    act_low = gelu_tanh(pre_act).astype(jnp.bfloat16)
    mlp_sum = lax.psum_scatter(
        jnp.dot(act_low, down_full, preferred_element_type=jnp.float32).astype(jnp.bfloat16),
        "tensor",
        scatter_dimension=0,
        tiled=True,
    ).astype(jnp.float32)
    output = (residual + mlp_sum + b_down).astype(jnp.bfloat16)
    grad_out = cotangent.astype(jnp.float32)
    down_bias_grad = jnp.sum(grad_out, axis=0)
    unused_act, gelu_pull = jax.vjp(gelu_tanh, pre_act)
    grad_rows = lax.all_gather(cotangent, "tensor", axis=0, tiled=True)
    down_grad = contract_rows(act_low, grad_rows)
    act_grad = contract_cols(grad_rows, down_full)
    pre_low = gelu_pull(act_grad)[0].astype(jnp.bfloat16)
    up_grad = contract_rows(rows_two, pre_low)
    up_bias_grad = place_slice(
        jnp.sum(pre_low, axis=0, dtype=jnp.float32), tensor_rank, b_up.shape[0]
    )
    norm_two_grad = lax.psum_scatter(
        contract_cols(pre_low, up_full).astype(jnp.bfloat16),
        "tensor",
        scatter_dimension=0,
        tiled=True,
    ).astype(jnp.float32)
    unused_two, norm_pull_two = jax.vjp(layer_norm, residual, gain_two, shift_two)
    residual_part, gain_two_grad, shift_two_grad = norm_pull_two(norm_two_grad)
    residual_grad = grad_out + residual_part
    branch_low = residual_grad.astype(jnp.bfloat16)
    out_bias_grad = jnp.sum(branch_low, axis=0, dtype=jnp.float32)
    branch_all = lax.all_gather(branch_low, "tensor", axis=0, tiled=True)
    query_back, key_back, value_back, out_back = (
        lax.all_gather(w_query.astype(jnp.bfloat16), "dp", axis=0, tiled=True),
        lax.all_gather(w_key.astype(jnp.bfloat16), "dp", axis=0, tiled=True),
        lax.all_gather(w_value.astype(jnp.bfloat16), "dp", axis=0, tiled=True),
        lax.all_gather(w_out.astype(jnp.bfloat16), "dp", axis=1, tiled=True),
    )
    out_grad = contract_rows(mixed_low, branch_all)
    mixed_grad = contract_cols(branch_all, out_back).astype(jnp.bfloat16)
    query_grads, key_grads, value_grads = lax.map(
        attend_backward,
        (
            by_image(queries_low),
            by_image(keys_low),
            by_image(values_low),
            by_image(mixed_grad),
            log_totals,
        ),
    )
    query_grads = query_grads.reshape(group_rows, head_cols)
    key_grads = key_grads.reshape(group_rows, head_cols)
    value_grads = value_grads.reshape(group_rows, head_cols)
    query_grad = contract_rows(rows_one, query_grads)
    key_grad = contract_rows(rows_one, key_grads)
    value_grad = contract_rows(rows_one, value_grads)
    query_bias_grad = place_slice(
        jnp.sum(query_grads, axis=0, dtype=jnp.float32), tensor_rank, b_query.shape[0]
    )
    value_bias_grad = place_slice(
        jnp.sum(value_grads, axis=0, dtype=jnp.float32), tensor_rank, b_value.shape[0]
    )
    norm_one_grad = lax.psum_scatter(
        (
            contract_cols(query_grads, query_back)
            + contract_cols(key_grads, key_back)
            + contract_cols(value_grads, value_back)
        ).astype(jnp.bfloat16),
        "tensor",
        scatter_dimension=0,
        tiled=True,
    ).astype(jnp.float32)
    unused_one, norm_pull_one = jax.vjp(layer_norm, inputs32, gain_one, shift_one)
    input_part, gain_one_grad, shift_one_grad = norm_pull_one(norm_one_grad)
    grad_tokens = (residual_grad + input_part).astype(jnp.bfloat16)
    query_grad, key_grad, value_grad, out_grad, up_grad, down_grad = (
        lax.psum_scatter(
            query_grad.astype(jnp.bfloat16), "dp", scatter_dimension=0, tiled=True
        ).astype(jnp.float32),
        lax.psum_scatter(
            key_grad.astype(jnp.bfloat16), "dp", scatter_dimension=0, tiled=True
        ).astype(jnp.float32),
        lax.psum_scatter(
            value_grad.astype(jnp.bfloat16), "dp", scatter_dimension=0, tiled=True
        ).astype(jnp.float32),
        lax.psum_scatter(
            out_grad.astype(jnp.bfloat16), "dp", scatter_dimension=1, tiled=True
        ).astype(jnp.float32),
        lax.psum_scatter(
            up_grad.astype(jnp.bfloat16), "dp", scatter_dimension=0, tiled=True
        ).astype(jnp.float32),
        lax.psum_scatter(
            down_grad.astype(jnp.bfloat16), "dp", scatter_dimension=1, tiled=True
        ).astype(jnp.float32),
    )
    small_sums = lax.psum(
        (
            gain_one_grad,
            shift_one_grad,
            query_bias_grad,
            value_bias_grad,
            out_bias_grad,
            gain_two_grad,
            shift_two_grad,
            up_bias_grad,
            down_bias_grad,
        ),
        ("dp", "tensor"),
    )
    return (
        output,
        grad_tokens,
        small_sums[0],
        small_sums[1],
        query_grad,
        small_sums[2],
        key_grad,
        value_grad,
        small_sums[3],
        out_grad,
        small_sums[4],
        small_sums[5],
        small_sums[6],
        up_grad,
        small_sums[7],
        down_grad,
        small_sums[8],
    )


def solution(mesh):
    return jax.shard_map(
        local,
        mesh=mesh,
        in_specs=(
            P(("dp", "tensor"), None),
            P(),
            P(),
            P("dp", "tensor"),
            P(),
            P("dp", "tensor"),
            P("dp", "tensor"),
            P(),
            P("tensor", "dp"),
            P(),
            P(),
            P(),
            P("dp", "tensor"),
            P(),
            P("tensor", "dp"),
            P(),
            P(("dp", "tensor"), None),
        ),
        out_specs=(
            P(("dp", "tensor"), None),
            P(("dp", "tensor"), None),
            P(),
            P(),
            P("dp", "tensor"),
            P(),
            P("dp", "tensor"),
            P("dp", "tensor"),
            P(),
            P("tensor", "dp"),
            P(),
            P(),
            P(),
            P("dp", "tensor"),
            P(),
            P("tensor", "dp"),
            P(),
        ),
        check_vma=False,
    )
```

profile of v0, /device:TPU:0, one launch (start us, length us, event | category | flops | bytes accessed | tf_op | source)
XLA Modules:
  0.0 1105.2 jit_solution(14938535337248682326)
XLA Ops:
  16.0 36.0 %all_gather.38 = bf16[288,1152]{0,1:T(8,128)(2,1)} all-gather(bf16[288,144]{0,1:T(8,128)(2,1)S(1)} %convert_element_type.170), channel_id=1, replica_groups=mesh['dp'=8,'tensor'=4] {'dp'}, dimensions={1}, use_global_device_ids=true | all-gather | bytes 746496 | tf_op jit(solution)/shard_map/all_gather | solution.py:141
  52.0 32.7 %all_gather.37 = bf16[1152,288]{1,0:T(8,128)(2,1)S(1)} all-gather(bf16[144,288]{1,0:T(8,128)(2,1)S(1)} %convert_element_type.168), channel_id=1, replica_groups=mesh['dp'=8,'tensor'=4] {'dp'}, dimensions={0}, use_global_device_ids=true | all-gather | bytes 746496 | tf_op jit(solution)/shard_map/all_gather | solution.py:140
  84.7 32.7 %all_gather.36 = bf16[1152,288]{1,0:T(8,128)(2,1)S(1)} all-gather(bf16[144,288]{1,0:T(8,128)(2,1)S(1)} %convert_element_type.166), channel_id=1, replica_groups=mesh['dp'=8,'tensor'=4] {'dp'}, dimensions={0}, use_global_device_ids=true | all-gather | bytes 746496 | tf_op jit(solution)/shard_map/all_gather | solution.py:139
  117.3 32.1 %all_gather.35 = bf16[1152,288]{1,0:T(8,128)(2,1)S(1)} all-gather(bf16[144,288]{1,0:T(8,128)(2,1)S(1)} %convert_element_type.164), channel_id=1, replica_groups=mesh['dp'=8,'tensor'=4] {'dp'}, dimensions={0}, use_global_device_ids=true | all-gather | bytes 746496 | tf_op jit(solution)/shard_map/all_gather | solution.py:138
  180.8 32.0 %while.54 = (s32[]{:T(128)}, bf16[2,1024,4,72]{3,2,1,0:T(4,128)(2,1)}, f32[2,2,4,512]{3,2,1,0:T(4,128)S(1)}, bf16[2,1024,4,72]{1,3,2,0:T(8,128)(2,1)}, bf16[2,10...) while((s32[]{:T(128)}, ...), condition=%wide.region_7.8_spmd, body=%wide.region_2.7_spmd.sunk | while | flops 622999552 | bytes 35750164 | solution.py:163
  184.0 10.8 while.57
  200.0 10.8 while.57
  227.5 46.3 %reduce-scatter.11.cloned.1.call-done = bf16[512,1152]{1,0:T(8,128)(2,1)} async-done(((bf16[2048,1152]{1,0:T(8,128)(2,1)}), bf16[512,1152]{1,0:T(8,128)(2,1)}) %reduce-scatter.11.cloned.1.call-update) | async-done | bytes 1179664 | tf_op jit(solution)/shard_map/reduce_scatter | solution.py:167
  284.4 37.4 %all-gather.15.cloned.1.call-done = bf16[2048,1152]{1,0:T(8,128)(2,1)} async-done(((bf16[512,1152]{1,0:T(8,128)(2,1)}), bf16[2048,1152]{1,0:T(8,128)(2,1)}) %all-gather.15.cloned.1.call-update) | async-done | bytes 4718608 | tf_op jit(solution)/shard_map/all_gather | solution.py:189
  321.8 11.1 %fusion.76 = f32[2048,1076]{0,1:T(8,128)} fusion(bf16[2048,1152]{1,0:T(8,128)(2,1)} %all-gather.15.cloned.1.call-done, bf16[1076,1152]{0,1:T(8,128)(2,1)} %all-gather.13.cloned.1.call-done), kind=kOutput, calls=%fused_computation.140 | convolution fusion | flops 5077204992 | bytes 16012288 | tf_op jit(solution)/shard_map/dot_general | solution.py:30
  332.9 46.8 %all-gather.11.cloned.1.call-done = bf16[1152,1076]{1,0:T(8,128)(2,1)} async-done(((bf16[144,1076]{1,0:T(8,128)(2,1)}), bf16[1152,1076]{1,0:T(8,128)(2,1)}) %all-gather.11.cloned.1.call-update) | async-done | bytes 2479120 | tf_op jit(solution)/shard_map/all_gather | solution.py:142
  379.7 38.1 %all-gather.9.cloned.1.call-done = bf16[2048,1152]{1,0:T(8,128)(2,1)} async-done(((bf16[512,1152]{1,0:T(8,128)(2,1)}), bf16[2048,1152]{1,0:T(8,128)(2,1)}) %all-gather.9.cloned.1.call-update) | async-done | bytes 4718608 | tf_op jit(solution)/shard_map/all_gather | solution.py:175
  417.9 20.3 %convert_reduce_fusion = (f32[1076]{0:T(1024)}, bf16[2048,1076]{0,1:T(8,128)(2,1)S(1)}, f32[2048,1076]{0,1:T(8,128)}) fusion(f32[2048,1076]{0,1:T(8,128)} %fusion.76, f32[1076]{0:T(1024)S(1)} %dynamic_slice.51, bf16[2048,1152]{1,0:T(8,128)(2,1)} %all-gather.9.cloned.1.call-done, bf16[1152,1076]{1,0:T(8,128)(2,1)} %all-gather.11.cloned.1.call-done), kind=kOutput, calls=%fused_computation.71 | convolution fusion | flops 5127887872 | bytes 29242784 | tf_op jit(solution)/shard_map/dot_general | solution.py:177
  440.3 8.9 convolution_convert_fusion.2
  449.2 13.1 %convolution_convert_fusion.3 = bf16[2048,1152]{1,0:T(8,128)(2,1)} fusion(bf16[1076,1152]{0,1:T(8,128)(2,1)} %all-gather.13.cloned.1.call-done, f32[2048,1076]{0,1:T(8,128)} %get-tuple-element.354), kind=kOutput, calls=%fused_computation.77 | convolution fusion | flops 5099397120 | bytes 16012288 | tf_op jit(solution)/shard_map/dot_general | solution.py:180
  462.4 34.8 %reduce-scatter.15.cloned.1.call-done = bf16[512,1152]{1,0:T(8,128)(2,1)} async-done(((bf16[2048,1152]{1,0:T(8,128)(2,1)}), bf16[512,1152]{1,0:T(8,128)(2,1)}) %reduce-scatter.15.cloned.1.call-update) | async-done | bytes 1179664 | tf_op jit(solution)/shard_map/reduce_scatter | solution.py:197
  500.8 46.6 %reduce-scatter.13.cloned.1.call-done = bf16[512,1152]{1,0:T(8,128)(2,1)} async-done(((bf16[2048,1152]{1,0:T(8,128)(2,1)}), bf16[512,1152]{1,0:T(8,128)(2,1)}) %reduce-scatter.13.cloned.1.call-update) | async-done | bytes 1179664 | tf_op jit(solution)/shard_map/reduce_scatter | solution.py:179
  554.0 13.0 %convolution_convert_fusion = bf16[1076,1152]{0,1:T(8,128)(2,1)} fusion(bf16[2048,1152]{1,0:T(8,128)(2,1)} %all-gather.15.cloned.1.call-done, f32[2048,1076]{0,1:T(8,128)} %get-tuple-element.354), kind=kOutput, calls=%fused_computation.74 | convolution fusion | flops 5098277376 | bytes 16012288 | tf_op jit(solution)/shard_map/dot_general | solution.py:24
  567.5 11.6 %convolution_convert_fusion.1 = bf16[1152,1076]{1,0:T(8,128)(2,1)} fusion(bf16[2048,1152]{1,0:T(8,128)(2,1)} %all-gather.9.cloned.1.call-done, bf16[2048,1076]{0,1:T(8,128)(2,1)} %copy-done.51), kind=kOutput, calls=%fused_computation.75 | convolution fusion | flops 5078444544 | bytes 11604992 | tf_op jit(solution)/shard_map/dot_general | solution.py:24
  579.2 11.9 %all-gather.17.cloned.1.call-done = bf16[2048,1152]{1,0:T(8,128)(2,1)} async-done(((bf16[512,1152]{1,0:T(8,128)(2,1)}), bf16[2048,1152]{1,0:T(8,128)(2,1)}) %all-gather.17.cloned.1.call-update) | async-done | bytes 4718608 | tf_op jit(solution)/shard_map/all_gather | solution.py:208
  605.6 76.4 %while.56 = (s32[]{:T(128)}, bf16[2,1024,4,72]{3,2,1,0:T(4,128)(2,1)}, bf16[2,1024,4,72]{1,3,2,0:T(8,128)(2,1)}, bf16[2,1024,4,72]{1,3,2,0:T(8,128)(2,1)}, bf16[...) while((s32[]{:T(128)}, ...), condition=%wide.region_19.20_spmd, body=%wide.region_15.19_spmd.sunk | while | flops 1537472512 | bytes 96657920 | solution.py:217
  613.4 24.2 %while.58 = (s32[]{:T(128)}, f32[1024,4,72]{0,2,1:T(8,128)S(1)}, f32[1024,4,72]{0,2,1:T(8,128)S(1)}, bf16[2,512,4,72]{1,3,2,0:T(8,128)(2,1)}, bf16[2,512,4,72]{1...) while((s32[]{:T(128)}, f32[1024,4,72]{0,2,1:T(8,128)S(1)}, ...), condition=%wide.region_18.18_spmd.clone, body=%wide.region_16.17_spmd.clone.sunk | while | flops 1536882688 | bytes 80371976 | solution.py:104
  651.6 24.2 %while.58 = (s32[]{:T(128)}, f32[1024,4,72]{0,2,1:T(8,128)S(1)}, f32[1024,4,72]{0,2,1:T(8,128)S(1)}, bf16[2,512,4,72]{1,3,2,0:T(8,128)(2,1)}, bf16[2,512,4,72]{1...) while((s32[]{:T(128)}, f32[1024,4,72]{0,2,1:T(8,128)S(1)}, ...), condition=%wide.region_18.18_spmd.clone, body=%wide.region_16.17_spmd.clone.sunk | while | flops 1536882688 | bytes 80371976 | solution.py:104
  687.6 6.0 convolution_convert_fusion.8
  695.4 6.1 convolution_convert_fusion.6
  725.5 14.3 %reduce-scatter.27.cloned.1.call-done = bf16[144,1076]{1,0:T(8,128)(2,1)} async-done(((bf16[1152,1076]{1,0:T(8,128)(2,1)}), bf16[144,1076]{1,0:T(8,128)(2,1)}) %reduce-scatter.27.cloned.1.call-update) | async-done | bytes 309904 | tf_op jit(solution)/shard_map/reduce_scatter | solution.py:265
  747.9 55.8 %reduce-scatter.25.cloned.1.call-done = bf16[288,144]{0,1:T(8,128)(2,1)} async-done(((bf16[288,1152]{0,1:T(8,128)(2,1)}), bf16[288,144]{0,1:T(8,128)(2,1)}) %reduce-scatter.25.cloned.1.call-update) | async-done | bytes 82960 | tf_op jit(solution)/shard_map/reduce_scatter | solution.py:262
  805.3 63.0 %reduce-scatter.19.cloned.1.call-done = bf16[144,288]{1,0:T(8,128)(2,1)} async-done(((bf16[1152,288]{1,0:T(8,128)(2,1)}), bf16[144,288]{1,0:T(8,128)(2,1)}) %reduce-scatter.19.cloned.1.call-update) | async-done | bytes 82960 | tf_op jit(solution)/shard_map/reduce_scatter | solution.py:253
  869.8 62.6 %reduce-scatter.23.cloned.1.call-done = bf16[144,288]{1,0:T(8,128)(2,1)} async-done(((bf16[1152,288]{1,0:T(8,128)(2,1)}), bf16[144,288]{1,0:T(8,128)(2,1)}) %reduce-scatter.23.cloned.1.call-update) | async-done | bytes 82960 | tf_op jit(solution)/shard_map/reduce_scatter | solution.py:259
  934.0 62.4 %reduce-scatter.21.cloned.1.call-done = bf16[144,288]{1,0:T(8,128)(2,1)} async-done(((bf16[1152,288]{1,0:T(8,128)(2,1)}), bf16[144,288]{1,0:T(8,128)(2,1)}) %reduce-scatter.21.cloned.1.call-update) | async-done | bytes 82960 | tf_op jit(solution)/shard_map/reduce_scatter | solution.py:256
  998.0 47.8 %reduce-scatter.17.cloned.1.call-done = bf16[512,1152]{1,0:T(8,128)(2,1)} async-done(((bf16[2048,1152]{1,0:T(8,128)(2,1)}), bf16[512,1152]{1,0:T(8,128)(2,1)}) %reduce-scatter.17.cloned.1.call-update) | async-done | bytes 1179664 | tf_op jit(solution)/shard_map/reduce_scatter | solution.py:239
  1055.1 42.5 %all-reduce = (f32[1152]{0:T(1024)}, f32[1152]{0:T(1024)}, f32[1152]{0:T(1024)}, f32[1152]{0:T(1024)}, f32[1152]{0:T(1024)}, /*index=5*/f32[1152]{0:T(1024)}, f32[1152]{0:T(1024)}, f32[4304]{0:T(1024)}, f32[1152]{0:T(1024)}) all-reduce(f32[1152]{0:T(1024)} %get-tuple-element.263, ...), channel_id=1, replica_groups=mesh['dp'=8,'tensor'=4] {'dp','tensor'}, use_global_device_ids=true, to_apply=%region_24.25 | all-reduce | flops 13520 | bytes 108160 | tf_op jit(solution)/shard_map/psum | solution.py:272
  (336 shorter events, 253.9 us)
Async XLA Ops:
  8.1 141.3 %all-gather.7.cloned.1.call-start = ((), (), s32[]{:S(2)}) async-start(), calls=%async_computation.10 | async-start | bytes 5898240 | tf_op jit(solution)/shard_map/all_gather | solution.py:149
  14.2 259.6 %reduce-scatter.11.cloned.1.call-start = ((), (), s32[]{:S(2)}) async-start(), calls=%async_computation.11 | async-start | bytes 5898240 | tf_op jit(solution)/shard_map/reduce_scatter | solution.py:167
  84.7 64.7 %copy-start.17 = (bf16[1152,288]{1,0:T(8,128)(2,1)}, bf16[1152,288]{1,0:T(8,128)(2,1)S(1)}, u32[]{:S(2)}) copy-start(bf16[1152,288]{1,0:T(8,128)(2,1)S(1)} %all_gather.37) | copy-start | bytes 1990660
  117.3 51.9 %copy-start.19 = (bf16[1152,288]{1,0:T(8,128)(2,1)}, bf16[1152,288]{1,0:T(8,128)(2,1)S(1)}, u32[]{:S(2)}) copy-start(bf16[1152,288]{1,0:T(8,128)(2,1)S(1)} %all_gather.36) | copy-start | bytes 1990660
  224.1 49.7 %copy-start.3 = (bf16[512,1152]{1,0:T(8,128)(2,1)S(1)}, bf16[512,1152]{1,0:T(8,128)(2,1)}, u32[]{:S(2)}) copy-start(bf16[512,1152]{1,0:T(8,128)(2,1)} %param.25) | copy-start | bytes 3538948
  224.2 49.7 %copy-start.32 = (f32[1152]{0:T(1024)S(1)}, f32[1152]{0:T(1024)}, u32[]{:S(2)}) copy-start(f32[1152]{0:T(1024)} %param.34) | copy-start | bytes 13828
  224.2 60.2 %all-gather.13.cloned.1.call-start = ((), (), s32[]{:S(2)}) async-start(), calls=%async_computation.14 | async-start | bytes 2985984 | tf_op jit(solution)/shard_map/all_gather | solution.py:143
  226.0 95.8 %all-gather.15.cloned.1.call-start = ((), (), s32[]{:S(2)}) async-start(), calls=%async_computation.16 | async-start | bytes 5898240 | tf_op jit(solution)/shard_map/all_gather | solution.py:189
  226.6 153.1 %all-gather.11.cloned.1.call-start = ((), (), s32[]{:S(2)}) async-start(), calls=%async_computation.13 | async-start | bytes 2985984 | tf_op jit(solution)/shard_map/all_gather | solution.py:142
  227.4 48.9 %copy-start.38 = (f32[1152]{0:T(1024)S(1)}, f32[1152]{0:T(1024)}, u32[]{:S(2)}) copy-start(f32[1152]{0:T(1024)} %param.35) | copy-start | bytes 13828
  227.4 48.9 %copy-start.48 = (f32[1152]{0:T(1024)S(1)}, f32[1152]{0:T(1024)}, u32[]{:S(2)}) copy-start(f32[1152]{0:T(1024)} %param.36) | copy-start | bytes 13828
  227.5 190.4 %all-gather.9.cloned.1.call-start = ((), (), s32[]{:S(2)}) async-start(), calls=%async_computation.12 | async-start | bytes 5898240 | tf_op jit(solution)/shard_map/all_gather | solution.py:175
  275.7 221.5 %copy-start.39 = (f32[512]{0:T(512)}, f32[512]{0:T(512)S(1)}, u32[]{:S(2)}) copy-start(f32[512]{0:T(512)S(1)} %broadcast_multiply_fusion) | copy-start | bytes 6148
  276.4 220.8 %copy-start.43 = (f32[512]{0:T(512)}, f32[512]{0:T(512)S(1)}, u32[]{:S(2)}) copy-start(f32[512]{0:T(512)S(1)} %fusion.72) | copy-start | bytes 6148
  278.1 219.1 %reduce-scatter.15.cloned.1.call-start = ((), (), s32[]{:S(2)}) async-start(), calls=%async_computation.17 | async-start | bytes 5898240 | tf_op jit(solution)/shard_map/reduce_scatter | solution.py:197
  417.9 22.4 %copy-start.50 = (bf16[1152,1076]{1,0:T(8,128)(2,1)S(1)}, bf16[1152,1076]{1,0:T(8,128)(2,1)}, u32[]{:S(2)}) copy-start(bf16[1152,1076]{1,0:T(8,128)(2,1)} %all-gather.11.cloned.1.call-done) | copy-start | bytes 7437316
  449.2 98.2 %reduce-scatter.13.cloned.1.call-start = ((), (), s32[]{:S(2)}) async-start(), calls=%async_computation.15 | async-start | bytes 5898240 | tf_op jit(solution)/shard_map/reduce_scatter | solution.py:179
  462.3 128.8 %all-gather.17.cloned.1.call-start = ((), (), s32[]{:S(2)}) async-start(), calls=%async_computation.18 | async-start | bytes 5898240 | tf_op jit(solution)/shard_map/all_gather | solution.py:208
  500.8 50.6 %copy-start.12 = (bf16[512,1152]{1,0:T(8,128)(2,1)S(1)}, bf16[512,1152]{1,0:T(8,128)(2,1)}, u32[]{:S(2)}) copy-start(bf16[512,1152]{1,0:T(8,128)(2,1)} %param.41) | copy-start | bytes 3538948
  553.7 169.8 %reduce-scatter.29.cloned.1.call-start = ((), (), s32[]{:S(2)}) async-start(), calls=%async_computation.25 | async-start | bytes 2985984 | tf_op jit(solution)/shard_map/reduce_scatter | solution.py:268
  567.1 172.8 %reduce-scatter.27.cloned.1.call-start = ((), (), s32[]{:S(2)}) async-start(), calls=%async_computation.24 | async-start | bytes 2985984 | tf_op jit(solution)/shard_map/reduce_scatter | solution.py:265
  579.1 224.6 %reduce-scatter.25.cloned.1.call-start = ((), (), s32[]{:S(2)}) async-start(), calls=%async_computation.23 | async-start | bytes 995328 | tf_op jit(solution)/shard_map/reduce_scatter | solution.py:262
  603.5 264.7 %reduce-scatter.19.cloned.1.call-start = ((), (), s32[]{:S(2)}) async-start(), calls=%async_computation.20 | async-start | bytes 995328 | tf_op jit(solution)/shard_map/reduce_scatter | solution.py:253
  693.6 238.8 %reduce-scatter.23.cloned.1.call-start = ((), (), s32[]{:S(2)}) async-start(), calls=%async_computation.22 | async-start | bytes 995328 | tf_op jit(solution)/shard_map/reduce_scatter | solution.py:259
  701.5 294.9 %reduce-scatter.21.cloned.1.call-start = ((), (), s32[]{:S(2)}) async-start(), calls=%async_computation.21 | async-start | bytes 995328 | tf_op jit(solution)/shard_map/reduce_scatter | solution.py:256
  712.1 333.7 %reduce-scatter.17.cloned.1.call-start = ((), (), s32[]{:S(2)}) async-start(), calls=%async_computation.19 | async-start | bytes 5898240 | tf_op jit(solution)/shard_map/reduce_scatter | solution.py:239
  741.7 304.1 %copy-start.4 = (bf16[512,1152]{1,0:T(8,128)(2,1)S(1)}, bf16[512,1152]{1,0:T(8,128)(2,1)}, u32[]{:S(2)}) copy-start(bf16[512,1152]{1,0:T(8,128)(2,1)} %param.25) | copy-start | bytes 3538948
  741.7 304.1 %copy-start.34 = (f32[1152]{0:T(1024)S(1)}, f32[1152]{0:T(1024)}, u32[]{:S(2)}) copy-start(f32[1152]{0:T(1024)} %param.26) | copy-start | bytes 13828
  741.7 304.1 %copy-start.37 = (f32[512]{0:T(512)S(1)}, f32[512]{0:T(512)}, u32[]{:S(2)}) copy-start(f32[512]{0:T(512)} %copy-done.36) | copy-start | bytes 6148
  745.5 303.7 %copy-start.41 = (f32[512]{0:T(512)S(1)}, f32[512]{0:T(512)}, u32[]{:S(2)}) copy-start(f32[512]{0:T(512)} %copy-done.40) | copy-start | bytes 6148
  747.9 248.5 %copy-start.42 = (f32[1152]{0:T(1024)}, f32[1152]{0:T(1024)S(1)}, u32[]{:S(2)}) copy-start(f32[1152]{0:T(1024)S(1)} %dynamic_update_slice.37) | copy-start | bytes 13828
  998.0 54.4 %copy-start.7 = (f32[512,1152]{1,0:T(8,128)S(1)}, f32[512,1152]{1,0:T(8,128)}, u32[]{:S(2)}) copy-start(f32[512,1152]{1,0:T(8,128)} %copy-done.6) | copy-start | bytes 7077892
  (50 other events, 203.2 us)
Sparse Core Ops, SparseCore 0:
  14.3 40.1 all-gather.6
  224.3 49.5 reduce-scatter.10
  449.3 47.8 reduce-scatter.14
  499.6 47.8 reduce-scatter.12
Sparse Core Ops, SparseCore 1:
  227.6 56.7 all-gather.12
  285.9 35.9 all-gather.14
  324.6 55.0 all-gather.10
  382.0 35.9 all-gather.8
  553.8 37.3 all-gather.16
  595.3 70.8 reduce-scatter.28
  669.6 70.1 reduce-scatter.26
  743.5 60.2 reduce-scatter.24
  807.9 60.3 reduce-scatter.18
  872.1 60.3 reduce-scatter.22
  936.1 60.2 reduce-scatter.20
  999.1 46.7 reduce-scatter.16
where the time goes:
time: 1120 us; the launch traced here: 1110 us
  waiting for transfers between devices  574 us (51%)
  matrix products  194 us (17%)
  blocking collectives  176 us (16%)
  local copies, waits for them, and re-layouts  80.8 us (7%)
  other arithmetic  61.4 us (5%)
  between operations  16.4 us (1%)
    reduce_scatter x1, waiting for transfers between devices, local(): lax.psum_scatter(query_grad.astype(jnp.bfloat16), 'dp', scatter_dimension...  63 us
    reduce_scatter x1, waiting for transfers between devices, local(): lax.psum_scatter(value_grad.astype(jnp.bfloat16), 'dp', scatter_dimension...  62.6 us
    reduce_scatter x1, waiting for transfers between devices, local(): lax.psum_scatter(key_grad.astype(jnp.bfloat16), 'dp', scatter_dimension=0...  62.4 us
    reduce_scatter x1, waiting for transfers between devices, local(): lax.psum_scatter(out_grad.astype(jnp.bfloat16), 'dp', scatter_dimension=1...  55.8 us
    reduce_scatter x1, waiting for transfers between devices, local(): lax.psum_scatter((contract_cols(query_grads, query_back) + contract_cols(...  47.8 us
    all_gather x1, waiting for transfers between devices, local(): lax.all_gather(w_up.astype(jnp.bfloat16), 'dp', axis=0, tiled=True)  46.8 us
    reduce_scatter x1, waiting for transfers between devices, local(): lax.psum_scatter(jnp.dot(act_low, down_full, preferred_element_type=jnp.f...  46.6 us
    reduce_scatter x1, waiting for transfers between devices, local(): lax.psum_scatter(jnp.dot(mixed_low, out_full, preferred_element_type=jnp....  46.3 us
  transfers between devices with their start and end apart: 16, of which 14 were waited for; matrix products, arithmetic and copies ran while one was open for 19% of the time, Pallas kernels for 0%

commit v1 on v0

v1 whole, which is shorter than its diff:
```python
import functools
import math

import jax
import jax.numpy as jnp
from jax import lax
from jax.experimental import pallas as pl
from jax.experimental.pallas import tpu as pltpu
from jax.sharding import PartitionSpec as P

HD = 72
LEN = 1024
NORM_EPS = 1e-06
LOW = jnp.bfloat16
F32 = jnp.float32
SCALE = HD ** (-0.5)
SCALE_LOG2 = SCALE * math.log2(math.e)
VMEM_LIMIT = 50 * 1024 * 1024

NN = (((1,), (0,)), ((), ()))
NT = (((1,), (1,)), ((), ()))
TN = (((0,), (0,)), ((), ()))


def dot(left, right, dims=NN):
    return lax.dot_general(left, right, dims, preferred_element_type=F32)


def layer_norm(values, norm_gain, norm_shift):
    centred = values - jnp.mean(values, axis=-1, keepdims=True)
    spread = jnp.mean(centred * centred, axis=-1, keepdims=True)
    return centred * lax.rsqrt(spread + NORM_EPS) * norm_gain + norm_shift


def gelu_tanh(values):
    return jax.nn.gelu(values, approximate=True)


def attend_forward_body(heads, block, qkv_ref, mixed_ref, lse_ref, q_s, k_s, vt_s, ot_s):
    cols = heads * HD
    for h in range(heads):
        lo = h * HD
        q_s[...] = qkv_ref[:, lo : lo + HD]
        k_s[...] = qkv_ref[:, cols + lo : cols + lo + HD]
        vt_s[...] = qkv_ref[:, 2 * cols + lo : 2 * cols + lo + HD].T

        def one_block(j, carry):
            at = pl.ds(pl.multiple_of(j * block, block), block)
            scores = dot(k_s[...], q_s[at, :], NT)
            highest = jnp.max(scores, axis=0, keepdims=True)
            probs = jnp.exp2((scores - highest) * SCALE_LOG2)
            total = jnp.sum(probs, axis=0, keepdims=True)
            mixed = dot(vt_s[...], probs.astype(LOW))
            ot_s[:, at] = mixed / total
            lse_ref[h : h + 1, at] = highest * SCALE_LOG2 + jnp.log2(total)
            return carry

        lax.fori_loop(0, LEN // block, one_block, 0)
        mixed_ref[:, lo : lo + HD] = ot_s[...].T.astype(LOW)


def attend_forward(qkv, heads):
    images, rows, _ = qkv.shape
    cols = heads * HD
    block = 256
    return pl.pallas_call(
        functools.partial(attend_forward_body, heads, block),
        grid=(images,),
        in_specs=[pl.BlockSpec((None, rows, 3 * cols), lambda i: (i, 0, 0))],
        out_specs=[
            pl.BlockSpec((None, rows, cols), lambda i: (i, 0, 0)),
            pl.BlockSpec((None, heads, rows), lambda i: (i, 0, 0)),
        ],
        out_shape=[
            jax.ShapeDtypeStruct((images, rows, cols), LOW),
            jax.ShapeDtypeStruct((images, heads, rows), F32),
        ],
        scratch_shapes=[
            pltpu.VMEM((rows, HD), LOW),
            pltpu.VMEM((rows, HD), LOW),
            pltpu.VMEM((HD, rows), LOW),
            pltpu.VMEM((HD, rows), F32),
        ],
        compiler_params=pltpu.CompilerParams(vmem_limit_bytes=VMEM_LIMIT),
        cost_estimate=pl.CostEstimate(
            flops=images * heads * rows * rows * 1024,
            bytes_accessed=images * rows * cols * 8,
            transcendentals=images * heads * rows * rows,
        ),
        name="attend_forward",
    )(qkv)


def attend_backward_body(
    heads, block, qkv_ref, grad_ref, mixed_ref, lse_ref, out_ref, q_s, k_s, v_s, do_s, kt_s, dqt_s, dk_s, dv_s, delta_s
):
    cols = heads * HD
    for h in range(heads):
        lo = h * HD
        q_s[...] = qkv_ref[:, lo : lo + HD]
        keys = qkv_ref[:, cols + lo : cols + lo + HD]
        k_s[...] = keys
        kt_s[...] = keys.T
        v_s[...] = qkv_ref[:, 2 * cols + lo : 2 * cols + lo + HD]
        grads = grad_ref[:, lo : lo + HD]
        do_s[...] = grads
        products = grads.astype(F32) * mixed_ref[:, lo : lo + HD].astype(F32)
        delta_s[...] = jnp.sum(products.T, axis=0, keepdims=True)
        dk_s[...] = jnp.zeros_like(dk_s)
        dv_s[...] = jnp.zeros_like(dv_s)

        def one_block(j, carry):
            at = pl.ds(pl.multiple_of(j * block, block), block)
            query = q_s[at, :]
            grad = do_s[at, :]
            scores = dot(k_s[...], query, NT)
            probs = jnp.exp2(scores * SCALE_LOG2 - lse_ref[h : h + 1, at])
            prob_grad = dot(v_s[...], grad, NT)
            dv_s[...] += dot(probs.astype(LOW), grad)
            score_grad = (probs * (prob_grad - delta_s[:, at])).astype(LOW)
            dk_s[...] += dot(score_grad, query)
            dqt_s[:, at] = dot(kt_s[...], score_grad)
            return carry

        lax.fori_loop(0, LEN // block, one_block, 0)
        out_ref[:, lo : lo + HD] = (dqt_s[...] * SCALE).T.astype(LOW)
        out_ref[:, cols + lo : cols + lo + HD] = (dk_s[...] * SCALE).astype(LOW)
        out_ref[:, 2 * cols + lo : 2 * cols + lo + HD] = dv_s[...].astype(LOW)


def attend_backward(qkv, grads, mixed, lse, heads):
    images, rows, _ = qkv.shape
    cols = heads * HD
    block = 256
    return pl.pallas_call(
        functools.partial(attend_backward_body, heads, block),
        grid=(images,),
        in_specs=[
            pl.BlockSpec((None, rows, 3 * cols), lambda i: (i, 0, 0)),
            pl.BlockSpec((None, rows, cols), lambda i: (i, 0, 0)),
            pl.BlockSpec((None, rows, cols), lambda i: (i, 0, 0)),
            pl.BlockSpec((None, heads, rows), lambda i: (i, 0, 0)),
        ],
        out_specs=pl.BlockSpec((None, rows, 3 * cols), lambda i: (i, 0, 0)),
        out_shape=jax.ShapeDtypeStruct((images, rows, 3 * cols), LOW),
        scratch_shapes=[
            pltpu.VMEM((rows, HD), LOW),
            pltpu.VMEM((rows, HD), LOW),
            pltpu.VMEM((rows, HD), LOW),
            pltpu.VMEM((rows, HD), LOW),
            pltpu.VMEM((HD, rows), LOW),
            pltpu.VMEM((HD, rows), F32),
            pltpu.VMEM((rows, HD), F32),
            pltpu.VMEM((rows, HD), F32),
            pltpu.VMEM((1, rows), F32),
        ],
        compiler_params=pltpu.CompilerParams(vmem_limit_bytes=VMEM_LIMIT),
        cost_estimate=pl.CostEstimate(
            flops=images * heads * rows * rows * 2560,
            bytes_accessed=images * rows * cols * 18,
            transcendentals=images * heads * rows * rows,
        ),
        name="attend_backward",
    )(qkv, grads, mixed, lse)


def place_body(count, first, table_ref, *refs):
    sources, out_ref, sem = refs[:-2], refs[-2], refs[-1]

    def piece(start, n):
        slot = table_ref[n]
        for at, source in enumerate(sources):
            @pl.when((slot >= at * first) & (slot < (at + 1) * first))
            def _():
                copy = pltpu.make_async_copy(source.at[slot - at * first], out_ref.at[n], sem.at[n])
                if start:
                    copy.start()
                else:
                    copy.wait()

    for n in range(count):
        piece(True, n)
    for n in range(count):
        piece(False, n)


def place(table, sources, name):
    first, *shape = sources[0].shape
    count = table.shape[0]
    if shape[0] % 16:
        return jnp.take(jnp.concatenate(sources, axis=0), table, axis=0)
    return pl.pallas_call(
        functools.partial(place_body, count, first),
        in_specs=[pl.BlockSpec(memory_space=pltpu.SMEM)] + [pl.BlockSpec(memory_space=pl.ANY)] * len(sources),
        out_specs=pl.BlockSpec(memory_space=pl.ANY),
        out_shape=jax.ShapeDtypeStruct((count, *shape), LOW),
        scratch_shapes=[pltpu.SemaphoreType.DMA((count,))],
        name=name,
    )(table, *sources)


class Plan:
    def __init__(self, n_dp, n_t, ranks):
        self.n_dp, self.n_t, self.ranks = n_dp, n_t, ranks
        self.images = n_t // ranks
        dims = [("dp", 1 << b) for b in reversed(range(n_dp.bit_length() - 1))]
        image_dims = [("image", 1 << b) for b in reversed(range(self.images.bit_length() - 1))]
        even = dims + image_dims
        odd = list(even)
        if image_dims and dims:
            odd[-2], odd[-1] = odd[-1], odd[-2]
        self.orders = (even, odd)
        self.stages = len(even)
        self.rank_stages = ranks.bit_length() - 1

    def permute(self, values, partner):
        pairs = []
        for d in range(self.n_dp):
            for t in range(self.n_t):
                d2, i2, r2 = partner(d, t // self.ranks, t % self.ranks)
                pairs.append((d * self.n_t + t, d2 * self.n_t + i2 * self.ranks + r2))
        return lax.ppermute(values, ("dp", "tensor"), pairs)

    def exchange(self, values, stage):
        def partner(d, i, r):
            kind, step = self.orders[r & 1][stage]
            return (d ^ step, i, r) if kind == "dp" else (d, i ^ step, r)

        return self.permute(values, partner)

    def rank_exchange(self, values, stage):
        return self.permute(values, lambda d, i, r: (d, i, r ^ (1 << stage)))

    def slots(self):
        me_dp, me_t = lax.axis_index("dp"), lax.axis_index("tensor")
        flips = jnp.arange(self.n_dp, dtype=jnp.int32)[None, :] ^ me_dp
        images = jnp.arange(self.images, dtype=jnp.int32)[:, None]

        def table(order):
            total = jnp.zeros((self.images, self.n_dp), jnp.int32)
            for stage, (kind, step) in enumerate(order):
                source = flips if kind == "dp" else images
                total = total + jnp.where((source & step) != 0, 1 << stage, 0)
            return total

        return jnp.where((me_t % self.ranks) & 1, table(self.orders[1]), table(self.orders[0]))

    def gather(self, shard):
        mine = shard[None]
        for stage in range(self.stages):
            theirs = self.exchange(mine, stage)
            if stage == self.stages - 1:
                return (mine, theirs)
            mine = jnp.concatenate([mine, theirs], axis=0)
        return (mine,)

    def scatter(self, pieces):
        for stage in reversed(range(self.stages)):
            half = pieces.shape[0] // 2
            theirs = self.exchange(pieces[half:], stage)
            total = pieces[:half].astype(F32) + theirs.astype(F32)
            pieces = total if stage == 0 else total.astype(LOW)
        return pieces[0]

    def rank_gather(self, shard):
        mine = shard
        for stage in range(self.rank_stages):
            mine = jnp.concatenate([mine, self.rank_exchange(mine, stage)], axis=0)
        return mine

    def rank_scatter(self, rows):
        for stage in reversed(range(self.rank_stages)):
            half = rows.shape[0] // 2
            theirs = self.rank_exchange(rows[half:].astype(LOW), stage)
            rows = rows[:half] + theirs.astype(F32)
        return rows


def local(
    tokens, gain_one, shift_one, w_query, b_query, w_key, w_value, b_value, w_out, b_out,
    gain_two, shift_two, w_up, b_up, w_down, b_down, cotangent, plan=None,
):
    images, ranks, n_dp = plan.images, plan.ranks, plan.n_dp
    shard_rows = w_query.shape[0]
    width = tokens.shape[1]
    head_cols, hidden_cols = w_query.shape[1], w_up.shape[1]
    heads = head_cols // HD
    me_t = lax.axis_index("tensor")
    me_image, me_rank = me_t // ranks, me_t % ranks
    slot_table = plan.slots().reshape(-1)
    piece_table = jnp.zeros_like(slot_table).at[slot_table].set(jnp.arange(slot_table.shape[0], dtype=jnp.int32))

    def shard_of(i):
        return (me_image ^ i) * ranks + me_rank

    def columns(vector, cols):
        return jnp.stack([lax.dynamic_slice_in_dim(vector, shard_of(i) * cols, cols) for i in range(images)])

    def uncolumns(parts, length):
        cols = parts.shape[1]
        blank = jnp.zeros((length,), F32)
        for i in range(images):
            blank = lax.dynamic_update_slice_in_dim(blank, parts[i], shard_of(i) * cols, 0)
        return blank

    def gathered(shard, name):
        full = place(slot_table, plan.gather(shard), name)
        return full.reshape(images, n_dp * shard_rows, shard.shape[1])

    def scattered(grads, name):
        pieces = jnp.concatenate(grads, axis=0).reshape(images * n_dp, shard_rows, -1)
        return plan.scatter(place(piece_table, [pieces], name))

    low = lambda v: v.astype(LOW)
    qkv_full = gathered(jnp.concatenate([low(w_query), low(w_key), low(w_value)], axis=1), "place_qkv")
    out_full = gathered(low(w_out).T, "place_out")
    up_full = gathered(low(w_up), "place_up")
    down_full = gathered(low(w_down).T, "place_down")

    cot_rows = plan.rank_gather(cotangent)
    inputs32 = tokens.astype(F32)
    normed_one = layer_norm(inputs32, gain_one, shift_one).astype(LOW)
    rows_one = plan.rank_gather(normed_one)
    qkv_bias = jnp.concatenate(
        [columns(b_query, head_cols), jnp.zeros((images, head_cols), F32), columns(b_value, head_cols)], axis=1
    )
    qkv = jnp.stack([low(dot(rows_one, qkv_full[i]) + qkv_bias[i]) for i in range(images)])
    mixed, lse = attend_forward(qkv, heads)

    attn = sum(dot(mixed[i], out_full[i], NT) for i in range(images))
    residual = inputs32 + plan.rank_scatter(attn) + b_out
    normed_two = layer_norm(residual, gain_two, shift_two).astype(LOW)
    rows_two = plan.rank_gather(normed_two)
    up_bias = columns(b_up, hidden_cols)
    pre_act, act = [], []
    for i in range(images):
        pre_act.append(dot(rows_two, up_full[i]) + up_bias[i])
        act.append(low(gelu_tanh(pre_act[i])))
    mlp = sum(dot(act[i], down_full[i], NT) for i in range(images))
    output = low(residual + plan.rank_scatter(mlp) + b_down)

    grad_out = cotangent.astype(F32)
    down_bias_grad = jnp.sum(grad_out, axis=0)
    pre_low, down_grads, up_grads, up_bias_parts = [], [], [], []
    for i in range(images):
        down_grads.append(low(dot(cot_rows, act[i], TN)))
        act_grad = dot(cot_rows, down_full[i])
        _, pull = jax.vjp(gelu_tanh, pre_act[i])
        pre_low.append(low(pull(act_grad)[0]))
        up_bias_parts.append(jnp.sum(pre_low[i], axis=0, dtype=F32))
        up_grads.append(low(dot(rows_two, pre_low[i], TN)))
    down_grad = scattered(down_grads, "place_grad_down").T
    up_grad = scattered(up_grads, "place_grad_up")
    up_bias_grad = uncolumns(jnp.stack(up_bias_parts), b_up.shape[0])
    norm_two_grad = plan.rank_scatter(sum(dot(pre_low[i], up_full[i], NT) for i in range(images)))
    _, pull_two = jax.vjp(layer_norm, residual, gain_two, shift_two)
    residual_part, gain_two_grad, shift_two_grad = pull_two(norm_two_grad)
    residual_grad = grad_out + residual_part
    branch_low = low(residual_grad)
    out_bias_grad = jnp.sum(branch_low, axis=0, dtype=F32)
    branch_rows = plan.rank_gather(branch_low)

    mixed_grad = jnp.stack([low(dot(branch_rows, out_full[i])) for i in range(images)])
    out_grad = scattered([low(dot(branch_rows, mixed[i], TN)) for i in range(images)], "place_grad_out").T
    qkv_grads = attend_backward(qkv, mixed_grad, mixed, lse, heads)
    qkv_grad = scattered([low(dot(rows_one, qkv_grads[i], TN)) for i in range(images)], "place_grad_qkv")
    query_grad, key_grad, value_grad = (qkv_grad[:, n * head_cols : (n + 1) * head_cols] for n in range(3))
    qkv_sums = jnp.sum(qkv_grads, axis=1, dtype=F32)
    query_bias_grad = uncolumns(qkv_sums[:, :head_cols], b_query.shape[0])
    value_bias_grad = uncolumns(qkv_sums[:, 2 * head_cols :], b_value.shape[0])
    norm_one_grad = plan.rank_scatter(sum(dot(qkv_grads[i], qkv_full[i], NT) for i in range(images)))
    _, pull_one = jax.vjp(layer_norm, inputs32, gain_one, shift_one)
    input_part, gain_one_grad, shift_one_grad = pull_one(norm_one_grad)
    grad_tokens = low(residual_grad + input_part)

    small = lax.psum(
        (
            gain_one_grad, shift_one_grad, query_bias_grad, value_bias_grad, out_bias_grad,
            gain_two_grad, shift_two_grad, up_bias_grad, down_bias_grad,
        ),
        ("dp", "tensor"),
    )
    return (
        output, grad_tokens, small[0], small[1], query_grad, small[2], key_grad, value_grad, small[3],
        out_grad, small[4], small[5], small[6], up_grad, small[7], down_grad, small[8],
    )


def solution(mesh):
    split = P(("dp", "tensor"), None)
    whole, wide, tall = P(), P("dp", "tensor"), P("tensor", "dp")
    n_dp, n_t = mesh.shape["dp"], mesh.shape["tensor"]

    def layer(*args):
        rows = args[0].shape[0] // (n_dp * n_t)
        plan = Plan(n_dp, n_t, LEN // rows)
        return jax.shard_map(
            functools.partial(local, plan=plan),
            mesh=mesh,
            in_specs=(
                split, whole, whole, wide, whole, wide, wide, whole, tall, whole,
                whole, whole, wide, whole, tall, whole, split,
            ),
            out_specs=(
                split, split, whole, whole, wide, whole, wide, wide, whole,
                tall, whole, whole, whole, wide, whole, tall, whole,
            ),
            check_vma=False,
        )(*args)

    return layer
```

time: 1120 us -> 1590 us (1.42)
  Pallas kernels: 0 us -> 1090 us
  waiting for transfers between devices: 574 us -> 158 us
  blocking collectives: 176 us -> 50.2 us
  matrix products: 194 us -> 103 us
  starting transfers between devices: 1.94 us -> 36 us
    pallas_call x0 -> x10, Pallas kernels: none -> 1090 us  [the longest x8 1020 us: place(): pl.pallas_call(functools.partial(place_body, count, first), in_specs=[pl....]
    reduce_scatter x10 -> x0, waiting for transfers between devices: 434 us -> none  [the longest x1 63 us: local(): lax.psum_scatter(query_grad.astype(jnp.bfloat16), 'dp', scatter_dimension...]
    ppermute x0 -> x40, waiting for transfers between devices: none -> 158 us  [permute(): return lax.ppermute(values, ('dp', 'tensor'), pairs)]
    all_gather x6 -> x0, waiting for transfers between devices: 140 us -> none  [the longest x1 46.8 us: local(): lax.all_gather(w_up.astype(jnp.bfloat16), 'dp', axis=0, tiled=True)]
    all_gather x4 -> x0, blocking collectives: 133 us -> none  [the longest x1 36 us: local(): lax.all_gather(w_out.astype(jnp.bfloat16), 'dp', axis=1, tiled=True)]
    dot_general x46 -> x24, matrix products: 194 us -> 103 us  [dot(): return lax.dot_general(left, right, dims, preferred_element_type=F32)]
    ppermute x0 -> x40, starting transfers between devices: none -> 36 us  [permute(): return lax.ppermute(values, ('dp', 'tensor'), pairs)]
    concatenate x0 -> x6, local copies, waits for them, and re-layouts: none -> 28.7 us  [the longest x4 26.3 us: scattered(): jnp.concatenate(grads, axis=0).reshape(images * n_dp, shard_rows, -1)]
  transfers between devices with their start and end apart: 16 -> 40, of which waited for: 14 -> 13; matrix products, arithmetic and copies ran while one was open for 19% -> 12% of each run, Pallas kernels for 0% -> 69%
where the time goes in v1:
time: 1590 us; the launch traced here: 1580 us
  Pallas kernels  1090 us (69%)
  waiting for transfers between devices  158 us (10%)
  matrix products  103 us (6%)
  other arithmetic  72.9 us (5%)
  local copies, waits for them, and re-layouts  70.3 us (4%)
  blocking collectives  50.2 us (3%)
  starting transfers between devices  36 us (2%)
    pallas_call x8, Pallas kernels, place(): pl.pallas_call(functools.partial(place_body, count, first), in_specs=[pl....  1020 us
    ppermute x40, waiting for transfers between devices, permute(): return lax.ppermute(values, ('dp', 'tensor'), pairs)  158 us
    dot_general x24, matrix products, dot(): return lax.dot_general(left, right, dims, preferred_element_type=F32)  103 us
    psum x1, blocking collectives, local(): lax.psum((gain_one_grad, shift_one_grad, query_bias_grad, value_bias_grad...  50.2 us
    pallas_call x1, Pallas kernels, attend_backward(): pl.pallas_call(functools.partial(attend_backward_body, heads, block), gri...  40.8 us
    ppermute x40, starting transfers between devices, permute(): return lax.ppermute(values, ('dp', 'tensor'), pairs)  36 us
  transfers between devices with their start and end apart: 40, of which 13 were waited for; matrix products, arithmetic and copies ran while one was open for 12% of the time, Pallas kernels for 69%

profile of v1, /device:TPU:0, one launch (start us, length us, event | category | flops | bytes accessed | tf_op | source)
XLA Modules:
  0.0 1581.2 jit_solution(4933012860267369839)
XLA Ops:
  12.9 25.5 %collective-permute-done.1 = bf16[1,144,864]{2,1,0:T(8,128)(2,1)S(1)} collective-permute-done((bf16[1,144,864]{2,1,0:T(8,128)(2,1)S(1)}, bf16[1,144,864]{2,1,0:T(8,128)(2,1)S(1)}, u32[]{:S(2)}, u32[]{:S(2)}) %collective-permute-start.1) | collective-permute-done | bytes 248864 | tf_op jit(solution)/shard_map/ppermute | solution.py:222
  40.2 22.4 %collective-permute-done.2 = bf16[2,144,864]{2,1,0:T(8,128)(2,1)S(1)} collective-permute-done((bf16[2,144,864]{2,1,0:T(8,128)(2,1)S(1)}, bf16[2,144,864]{2,1,0:T(8,128)(2,1)S(1)}, u32[]{:S(2)}, u32[]{:S(2)}) %collective-permute-start.2) | collective-permute-done | bytes 497696 | tf_op jit(solution)/shard_map/ppermute | solution.py:222
  67.7 6.1 collective-permute-done.6
  82.0 6.0 collective-permute-done.12
  94.6 6.5 collective-permute-done.16
  103.7 26.3 %collective-permute-done.8.refs_1_ = bf16[8,144,288]{2,1,0:T(8,128)(2,1)} collective-permute-done((bf16[8,144,288]{2,1,0:T(8,128)(2,1)}, bf16[8,144,288]{2,1,0:T(8,128)(2,1)}, u32[]{:S(2)}, u32[]{:S(2)}) %collective-permute-start.8) | collective-permute-done | bytes 663584 | tf_op jit(solution)/shard_map/ppermute | solution.py:222
  131.4 55.5 %place_out.1 = bf16[16,144,288]{2,1,0:T(8,128)(2,1)} custom-call(s32[16]{0:T(128)} %select_n.126.table_ref, bf16[8,144,288]{2,1,0:T(8,128)(2,1)} %pad_maximum_fusion.15.refs_0_, bf16[8,144,288]{2,1,0:T(8,128)(2,1)} %collective-permute-done.8.refs_1_), custom_call_target="tpu_custom_call" | custom-call | tf_op jit(solution)/shard_map/place_out/pallas_call | solution.py:192
  194.8 127.0 %place_qkv.1 = bf16[16,144,864]{2,1,0:T(8,128)(2,1)} custom-call(s32[16]{0:T(128)} %select_n.126.table_ref, bf16[8,144,864]{2,1,0:T(8,128)(2,1)} %copy-done.12, bf16[8,144,864]{2,1,0:T(8,128)(2,1)} %collective-permute-done.4.refs_1_), custom_call_target="tpu_custom_call" | custom-call | tf_op jit(solution)/shard_map/place_qkv/pallas_call | solution.py:192
  324.3 5.9 fusion.30
  337.1 31.1 %attend_forward.1 = (bf16[2,1024,288]{2,1,0:T(8,128)(2,1)S(1)}, f32[2,4,1024]{2,1,0:T(4,128)S(1)}) custom-call(bf16[2,1024,864]{2,1,0:T(8,128)(2,1)} %pad_maximum_fusion.3.qkv_ref), custom_call_target="tpu_custom_call" | custom-call | flops 8589934592 | bytes 4718592 | tf_op jit(solution)/shard_map/attend_forward/pallas_call | solution.py:66
  384.3 162.7 %place_up.1 = bf16[16,144,1076]{2,1,0:T(8,128)(2,1)} custom-call(s32[16]{0:T(128)} %select_n.126.table_ref, bf16[8,144,1076]{2,1,0:T(8,128)(2,1)} %pad_maximum_fusion.4.refs_0_, bf16[8,144,1076]{2,1,0:T(8,128)(2,1)} %collective-permute-done.14.refs_1_), custom_call_target="tpu_custom_call" | custom-call | tf_op jit(solution)/shard_map/place_up/pallas_call | solution.py:192
  555.7 162.7 %place_down.1 = bf16[16,144,1076]{2,1,0:T(8,128)(2,1)} custom-call(s32[16]{0:T(128)} %select_n.126.table_ref, bf16[8,144,1076]{2,1,0:T(8,128)(2,1)} %pad_maximum_fusion.5.refs_0_, bf16[8,144,1076]{2,1,0:T(8,128)(2,1)} %collective-permute-done.18.refs_1_), custom_call_target="tpu_custom_call" | custom-call | tf_op jit(solution)/shard_map/place_down/pallas_call | solution.py:192
  730.6 7.5 convert_reduce_fusion.1
  746.4 8.6 convert_reduce_fusion.2
  776.7 7.8 convolution_convert_fusion
  792.2 6.2 convolution_convert_fusion.1
  798.3 8.5 copy.40
  806.8 5.1 pad_maximum_fusion.1
  811.9 8.6 copy.41
  820.5 162.7 %place_grad_up.1 = bf16[16,144,1076]{2,1,0:T(8,128)(2,1)} custom-call(s32[16]{0:T(128)} %scatter_custom_fusion.table_ref, bf16[16,144,1076]{2,1,0:T(8,128)(2,1)} %bitcast.91), custom_call_target="tpu_custom_call" | custom-call | tf_op jit(solution)/shard_map/place_grad_up/pallas_call | solution.py:192
  983.3 162.7 %place_grad_down.1 = bf16[16,144,1076]{2,1,0:T(8,128)(2,1)} custom-call(s32[16]{0:T(128)} %scatter_custom_fusion.table_ref, bf16[16,144,1076]{2,1,0:T(8,128)(2,1)} %bitcast.92), custom_call_target="tpu_custom_call" | custom-call | tf_op jit(solution)/shard_map/place_grad_down/pallas_call | solution.py:192
  1162.4 55.6 %place_grad_out.1 = bf16[16,144,288]{2,1,0:T(8,128)(2,1)} custom-call(s32[16]{0:T(128)} %scatter_custom_fusion.table_ref, bf16[16,144,288]{2,1,0:T(8,128)(2,1)} %bitcast.96), custom_call_target="tpu_custom_call" | custom-call | tf_op jit(solution)/shard_map/place_grad_out/pallas_call | solution.py:192
  1228.0 40.8 %attend_backward.1 = bf16[2,1024,864]{2,1,0:T(8,128)(2,1)} custom-call(bf16[2,1024,864]{2,1,0:T(8,128)(2,1)} %pad_maximum_fusion.3.qkv_ref, bf16[2,1024,288]{2,1,0:T(8,128)(2,1)S(1)} %pad_maximum_fusion.10.grad_ref, bf16[2,1024,288]{2,1,0:T(8,128)(2,1)S(1)} %get-tuple-element.19.mixed_ref, f32[2,4,1024]{2,1,0:T(4,128)S(1)} %get-tuple-element.20.lse_ref), custom_call_target="tpu_custom_call" | custom-call | flops 21474836480 | bytes 10616832 | tf_op jit(solution)/shard_map/attend_backward/pallas_call | solution.py:135
  1268.8 4.9 convolution_convert_fusion.4
  1280.1 6.5 copy.38
  1286.6 127.1 %place_grad_qkv.1 = bf16[16,144,864]{2,1,0:T(8,128)(2,1)} custom-call(s32[16]{0:T(128)} %scatter_custom_fusion.table_ref, bf16[16,144,864]{2,1,0:T(8,128)(2,1)} %bitcast.93), custom_call_target="tpu_custom_call" | custom-call | tf_op jit(solution)/shard_map/place_grad_qkv/pallas_call | solution.py:192
  1435.5 6.7 collective-permute-done.29
  1458.8 50.2 %all-reduce = (f32[1152]{0:T(1024)}, f32[1152]{0:T(1024)}, f32[1152]{0:T(1024)}, f32[1152]{0:T(1024)}, f32[1152]{0:T(1024)}, /*index=5*/f32[1152]{0:T(1024)}, f32[1152]{0:T(1024)}, f32[4304]{0:T(1024)}, f32[1152]{0:T(1024)}) all-reduce(f32[1152]{0:T(1024)S(1)} %get-tuple-element.23, ...), channel_id=1, replica_groups=mesh['dp'=8,'tensor'=4] {'dp','tensor'}, use_global_device_ids=true, to_apply=%region_9.10 | all-reduce | flops 13520 | bytes 108160 | tf_op jit(solution)/shard_map/psum | solution.py:376
  1519.7 13.4 collective-permute-done.34
  1533.3 15.4 collective-permute-done.38
  1552.5 15.9 %collective-permute-done.26 = bf16[2,144,864]{2,1,0:T(8,128)(2,1)S(1)} collective-permute-done((bf16[2,144,864]{2,1,0:T(8,128)(2,1)S(1)}, bf16[2,144,864]{2,1,0:T(8,128)(2,1)S(1)}, u32[]{:S(2)}, u32[]{:S(2)}) %collective-permute-start.26) | collective-permute-done | bytes 497696 | tf_op jit(solution)/shard_map/ppermute | solution.py:222
  1569.8 10.1 collective-permute-done.27
  (364 shorter events, 216.4 us)
Async XLA Ops:
  1.8 63.5 %collective-permute-start.5 = (bf16[1,144,288]{2,1,0:T(8,128)(2,1)S(1)}, bf16[1,144,288]{2,1,0:T(8,128)(2,1)S(1)}, u32[]{:S(2)}, u32[]{:S(2)}) collective-permute-start(bf16[1,144,288]{2,1,0:T(8,128)(2,1)S(1)} %convert_bitcast_fusion.2), channel_id=1, source_target_pairs={{0,16},{1,17},{2,18},{3,19},{4,20},{5,21},{6,22},{7,23},{8,24},{9,... | collective-permute-start | bytes 248840 | tf_op jit(solution)/shard_map/ppermute | solution.py:222
  8.9 29.6 %collective-permute-start.1 = (bf16[1,144,864]{2,1,0:T(8,128)(2,1)S(1)}, bf16[1,144,864]{2,1,0:T(8,128)(2,1)S(1)}, u32[]{:S(2)}, u32[]{:S(2)}) collective-permute-start(bf16[1,144,864]{2,1,0:T(8,128)(2,1)S(1)} %maximum_bitcast_fusion), channel_id=1, source_target_pairs={{0,16},{1,17},{2,18},{3,19},{4,20},{5,21},{6,22},{7,23},{8,24},{9,... | collective-permute-start | bytes 746504 | tf_op jit(solution)/shard_map/ppermute | solution.py:222
  9.1 66.1 %collective-permute-start.15 = (bf16[1,144,1076]{2,1,0:T(8,128)(2,1)S(1)}, bf16[1,144,1076]{2,1,0:T(8,128)(2,1)S(1)}, u32[]{:S(2)}, u32[]{:S(2)}) collective-permute-start(bf16[1,144,1076]{2,1,0:T(8,128)(2,1)S(1)} %convert_bitcast_fusion), channel_id=1, source_target_pairs={{0,16},{1,17},{2,18},{3,19},{4,20},{5,21},{6,22},{7,23},{8,24},{9,... | collective-permute-start | bytes 929672 | tf_op jit(solution)/shard_map/ppermute | solution.py:222
  12.1 53.4 %collective-permute-start.11 = (bf16[1,144,1076]{2,1,0:T(8,128)(2,1)S(1)}, bf16[1,144,1076]{2,1,0:T(8,128)(2,1)S(1)}, u32[]{:S(2)}, u32[]{:S(2)}) collective-permute-start(bf16[1,144,1076]{2,1,0:T(8,128)(2,1)S(1)} %convert_bitcast_fusion.1), channel_id=1, source_target_pairs={{0,16},{1,17},{2,18},{3,19},{4,20},{5,21},{6,22},{7,23},{8,24},{9,... | collective-permute-start | bytes 929672 | tf_op jit(solution)/shard_map/ppermute | solution.py:222
  38.5 24.0 %collective-permute-start.2 = (bf16[2,144,864]{2,1,0:T(8,128)(2,1)S(1)}, bf16[2,144,864]{2,1,0:T(8,128)(2,1)S(1)}, u32[]{:S(2)}, u32[]{:S(2)}) collective-permute-start(bf16[2,144,864]{2,1,0:T(8,128)(2,1)S(1)} %pad_maximum_fusion.18), channel_id=1, source_target_pairs={{0,8},{1,9},{2,10},{3,11},{4,12},{5,13},{6,14},{7,15},{8,0},{9,1},... | collective-permute-start | bytes 1493000 | tf_op jit(solution)/shard_map/ppermute | solution.py:222
  40.2 284.2 %collective-permute-start = (bf16[512,1152]{1,0:T(8,128)(2,1)}, bf16[512,1152]{1,0:T(8,128)(2,1)}, u32[]{:S(2)}, u32[]{:S(2)}) collective-permute-start(bf16[512,1152]{1,0:T(8,128)(2,1)} %fusion.21), channel_id=1, source_target_pairs={{0,1},{1,0},{2,3},{3,2},{4,5},{5,4},{6,7},{7,6},{8,9},{9,8},{10,11... | collective-permute-start | bytes 3538952 | tf_op jit(solution)/shard_map/ppermute | solution.py:222
  65.6 22.4 %collective-permute-start.12 = (bf16[2,144,1076]{2,1,0:T(8,128)(2,1)S(1)}, bf16[2,144,1076]{2,1,0:T(8,128)(2,1)S(1)}, u32[]{:S(2)}, u32[]{:S(2)}) collective-permute-start(bf16[2,144,1076]{2,1,0:T(8,128)(2,1)S(1)} %pad_maximum_fusion.16), channel_id=1, source_target_pairs={{0,8},{1,9},{2,10},{3,11},{4,12},{5,13},{6,14},{7,15},{8,0},{9,1},... | collective-permute-start | bytes 1859336 | tf_op jit(solution)/shard_map/ppermute | solution.py:222
  76.1 25.0 %collective-permute-start.16 = (bf16[2,144,1076]{2,1,0:T(8,128)(2,1)}, bf16[2,144,1076]{2,1,0:T(8,128)(2,1)}, u32[]{:S(2)}, u32[]{:S(2)}) collective-permute-start(bf16[2,144,1076]{2,1,0:T(8,128)(2,1)} %pad_maximum_fusion.17), channel_id=1, source_target_pairs={{0,8},{1,9},{2,10},{3,11},{4,12},{5,13},{6,14},{7,15},{8,0},{9,1},... | collective-permute-start | bytes 1859336 | tf_op jit(solution)/shard_map/ppermute | solution.py:222
  80.4 114.4 %collective-permute-start.4 = (bf16[8,144,864]{2,1,0:T(8,128)(2,1)S(1)}, bf16[8,144,864]{2,1,0:T(8,128)(2,1)}, u32[]{:S(2)}, u32[]{:S(2)}) collective-permute-start(bf16[8,144,864]{2,1,0:T(8,128)(2,1)S(1)} %pad_maximum_fusion.9.refs_0_), channel_id=1, source_target_pairs={{0,2},{1,5},{2,0},{3,7},{4,6},{5,1},{6,4},{7,3},{8,10},{9,13},{10,... | collective-permute-start | bytes 5971976 | tf_op jit(solution)/shard_map/ppermute | solution.py:222
  89.3 100.6 %collective-permute-start.13 = (bf16[4,144,1076]{2,1,0:T(8,128)(2,1)}, bf16[4,144,1076]{2,1,0:T(8,128)(2,1)}, u32[]{:S(2)}, u32[]{:S(2)}) collective-permute-start(bf16[4,144,1076]{2,1,0:T(8,128)(2,1)} %pad_maximum_fusion.11), channel_id=1, source_target_pairs={{0,4},{1,3},{2,6},{3,1},{4,0},{5,7},{6,2},{7,5},{8,12},{9,11},{10,... | collective-permute-start | bytes 3718664 | tf_op jit(solution)/shard_map/ppermute | solution.py:222
  92.1 37.9 %collective-permute-start.8 = (bf16[8,144,288]{2,1,0:T(8,128)(2,1)}, bf16[8,144,288]{2,1,0:T(8,128)(2,1)}, u32[]{:S(2)}, u32[]{:S(2)}) collective-permute-start(bf16[8,144,288]{2,1,0:T(8,128)(2,1)} %pad_maximum_fusion.15.refs_0_), channel_id=1, source_target_pairs={{0,2},{1,5},{2,0},{3,7},{4,6},{5,1},{6,4},{7,3},{8,10},{9,13},{10,... | collective-permute-start | bytes 1990664 | tf_op jit(solution)/shard_map/ppermute | solution.py:222
  101.1 277.2 %collective-permute-start.20 = (bf16[512,1152]{1,0:T(8,128)(2,1)}, bf16[512,1152]{1,0:T(8,128)(2,1)}, u32[]{:S(2)}, u32[]{:S(2)}) collective-permute-start(bf16[512,1152]{1,0:T(8,128)(2,1)} %param.33), channel_id=1, source_target_pairs={{0,1},{1,0},{2,3},{3,2},{4,5},{5,4},{6,7},{7,6},{8,9},{9,8},{10,11... | collective-permute-start | bytes 3538952 | tf_op jit(solution)/shard_map/ppermute | solution.py:222
  129.9 250.8 %collective-permute-start.17 = (bf16[4,144,1076]{2,1,0:T(8,128)(2,1)}, bf16[4,144,1076]{2,1,0:T(8,128)(2,1)}, u32[]{:S(2)}, u32[]{:S(2)}) collective-permute-start(bf16[4,144,1076]{2,1,0:T(8,128)(2,1)} %pad_maximum_fusion.12), channel_id=1, source_target_pairs={{0,4},{1,3},{2,6},{3,1},{4,0},{5,7},{6,2},{7,5},{8,12},{9,11},{10,... | collective-permute-start | bytes 3718664 | tf_op jit(solution)/shard_map/ppermute | solution.py:222
  193.3 191.0 %collective-permute-start.14 = (bf16[8,144,1076]{2,1,0:T(8,128)(2,1)}, bf16[8,144,1076]{2,1,0:T(8,128)(2,1)}, u32[]{:S(2)}, u32[]{:S(2)}) collective-permute-start(bf16[8,144,1076]{2,1,0:T(8,128)(2,1)} %pad_maximum_fusion.4.refs_0_), channel_id=1, source_target_pairs={{0,2},{1,5},{2,0},{3,7},{4,6},{5,1},{6,4},{7,3},{8,10},{9,13},{10,... | collective-permute-start | bytes 7437320 | tf_op jit(solution)/shard_map/ppermute | solution.py:222
  374.6 172.4 %collective-permute-start.9 = (bf16[512,1152]{1,0:T(8,128)(2,1)}, bf16[512,1152]{1,0:T(8,128)(2,1)}, u32[]{:S(2)}, u32[]{:S(2)}) collective-permute-start(bf16[512,1152]{1,0:T(8,128)(2,1)} %slice.412), channel_id=1, source_target_pairs={{0,1},{1,0},{2,3},{3,2},{4,5},{5,4},{6,7},{7,6},{8,9},{9,8},{10,11... | collective-permute-start | bytes 3538952 | tf_op jit(solution)/shard_map/ppermute | solution.py:222
  383.8 171.9 %collective-permute-start.18 = (bf16[8,144,1076]{2,1,0:T(8,128)(2,1)}, bf16[8,144,1076]{2,1,0:T(8,128)(2,1)}, u32[]{:S(2)}, u32[]{:S(2)}) collective-permute-start(bf16[8,144,1076]{2,1,0:T(8,128)(2,1)} %pad_maximum_fusion.5.refs_0_), channel_id=1, source_target_pairs={{0,2},{1,5},{2,0},{3,7},{4,6},{5,1},{6,4},{7,3},{8,10},{9,13},{10,... | collective-permute-start | bytes 7437320 | tf_op jit(solution)/shard_map/ppermute | solution.py:222
  551.1 170.5 %collective-permute-start.10 = (bf16[512,1152]{1,0:T(8,128)(2,1)S(1)}, bf16[512,1152]{1,0:T(8,128)(2,1)}, u32[]{:S(2)}, u32[]{:S(2)}) collective-permute-start(bf16[512,1152]{1,0:T(8,128)(2,1)S(1)} %add_convert_fusion.8), channel_id=1, source_target_pairs={{0,1},{1,0},{2,3},{3,2},{4,5},{5,4},{6,7},{7,6},{8,9},{9,8},{10,11... | collective-permute-start | bytes 3538952 | tf_op jit(solution)/shard_map/ppermute | solution.py:222
  763.4 22.1 %collective-permute-start.19 = (bf16[512,1152]{1,0:T(8,128)(2,1)S(1)}, bf16[512,1152]{1,0:T(8,128)(2,1)}, u32[]{:S(2)}, u32[]{:S(2)}) collective-permute-start(bf16[512,1152]{1,0:T(8,128)(2,1)S(1)} %slice.411), channel_id=1, source_target_pairs={{0,1},{1,0},{2,3},{3,2},{4,5},{5,4},{6,7},{7,6},{8,9},{9,8},{10,11... | collective-permute-start | bytes 3538952 | tf_op jit(solution)/shard_map/ppermute | solution.py:222
  763.8 20.8 %collective-permute-start.21 = (bf16[512,1152]{1,0:T(8,128)(2,1)S(1)}, bf16[512,1152]{1,0:T(8,128)(2,1)S(1)}, u32[]{:S(2)}, u32[]{:S(2)}) collective-permute-start(bf16[512,1152]{1,0:T(8,128)(2,1)S(1)} %slice.410), channel_id=1, source_target_pairs={{0,1},{1,0},{2,3},{3,2},{4,5},{5,4},{6,7},{7,6},{8,9},{9,8},{10,11... | collective-permute-start | bytes 3538952 | tf_op jit(solution)/shard_map/ppermute | solution.py:222
  791.8 362.3 %collective-permute-start.22 = (bf16[512,1152]{1,0:T(8,128)(2,1)S(1)}, bf16[512,1152]{1,0:T(8,128)(2,1)}, u32[]{:S(2)}, u32[]{:S(2)}) collective-permute-start(bf16[512,1152]{1,0:T(8,128)(2,1)S(1)} %get-tuple-element.47), channel_id=1, source_target_pairs={{0,1},{1,0},{2,3},{3,2},{4,5},{5,4},{6,7},{7,6},{8,9},{9,8},{10,11... | collective-permute-start | bytes 3538952 | tf_op jit(solution)/shard_map/ppermute | solution.py:222
  1151.6 278.9 %collective-permute-start.32 = (bf16[8,144,1076]{2,1,0:T(8,128)(2,1)}, bf16[8,144,1076]{2,1,0:T(8,128)(2,1)}, u32[]{:S(2)}, u32[]{:S(2)}) collective-permute-start(bf16[8,144,1076]{2,1,0:T(8,128)(2,1)} %slice.318), channel_id=1, source_target_pairs={{0,2},{1,5},{2,0},{3,7},{4,6},{5,1},{6,4},{7,3},{8,10},{9,13},{10,... | collective-permute-start | bytes 7437320 | tf_op jit(solution)/shard_map/ppermute | solution.py:222
  1153.1 289.3 %collective-permute-start.36 = (bf16[8,144,1076]{2,1,0:T(8,128)(2,1)}, bf16[8,144,1076]{2,1,0:T(8,128)(2,1)}, u32[]{:S(2)}, u32[]{:S(2)}) collective-permute-start(bf16[8,144,1076]{2,1,0:T(8,128)(2,1)} %slice.326), channel_id=1, source_target_pairs={{0,2},{1,5},{2,0},{3,7},{4,6},{5,1},{6,4},{7,3},{8,10},{9,13},{10,... | collective-permute-start | bytes 7437320 | tf_op jit(solution)/shard_map/ppermute | solution.py:222
  1220.3 207.1 %collective-permute-start.28 = (bf16[8,144,288]{2,1,0:T(8,128)(2,1)}, bf16[8,144,288]{2,1,0:T(8,128)(2,1)}, u32[]{:S(2)}, u32[]{:S(2)}) collective-permute-start(bf16[8,144,288]{2,1,0:T(8,128)(2,1)} %slice.310), channel_id=1, source_target_pairs={{0,2},{1,5},{2,0},{3,7},{4,6},{5,1},{6,4},{7,3},{8,10},{9,13},{10,... | collective-permute-start | bytes 1990664 | tf_op jit(solution)/shard_map/ppermute | solution.py:222
  1416.9 98.5 %collective-permute-start.24 = (bf16[8,144,864]{2,1,0:T(8,128)(2,1)}, bf16[8,144,864]{2,1,0:T(8,128)(2,1)}, u32[]{:S(2)}, u32[]{:S(2)}) collective-permute-start(bf16[8,144,864]{2,1,0:T(8,128)(2,1)} %slice.295), channel_id=1, source_target_pairs={{0,2},{1,5},{2,0},{3,7},{4,6},{5,1},{6,4},{7,3},{8,10},{9,13},{10,... | collective-permute-start | bytes 5971976 | tf_op jit(solution)/shard_map/ppermute | solution.py:222
  1424.7 26.3 %collective-permute-start.23 = (bf16[512,1152]{1,0:T(8,128)(2,1)}, bf16[512,1152]{1,0:T(8,128)(2,1)}, u32[]{:S(2)}, u32[]{:S(2)}) collective-permute-start(bf16[512,1152]{1,0:T(8,128)(2,1)} %slice.409), channel_id=1, source_target_pairs={{0,1},{1,0},{2,3},{3,2},{4,5},{5,4},{6,7},{7,6},{8,9},{9,8},{10,11... | collective-permute-start | bytes 3538952 | tf_op jit(solution)/shard_map/ppermute | solution.py:222
  1434.8 74.9 %collective-permute-start.33 = (bf16[4,144,1076]{2,1,0:T(8,128)(2,1)}, bf16[4,144,1076]{2,1,0:T(8,128)(2,1)}, u32[]{:S(2)}, u32[]{:S(2)}) collective-permute-start(bf16[4,144,1076]{2,1,0:T(8,128)(2,1)} %slice.320), channel_id=1, source_target_pairs={{0,4},{1,3},{2,6},{3,1},{4,0},{5,7},{6,2},{7,5},{8,12},{9,11},{10,... | collective-permute-start | bytes 3718664 | tf_op jit(solution)/shard_map/ppermute | solution.py:222
  1446.4 65.3 %collective-permute-start.37 = (bf16[4,144,1076]{2,1,0:T(8,128)(2,1)}, bf16[4,144,1076]{2,1,0:T(8,128)(2,1)}, u32[]{:S(2)}, u32[]{:S(2)}) collective-permute-start(bf16[4,144,1076]{2,1,0:T(8,128)(2,1)} %slice.328), channel_id=1, source_target_pairs={{0,4},{1,3},{2,6},{3,1},{4,0},{5,7},{6,2},{7,5},{8,12},{9,11},{10,... | collective-permute-start | bytes 3718664 | tf_op jit(solution)/shard_map/ppermute | solution.py:222
  1449.0 60.0 %collective-permute-start.31 = (bf16[1,144,288]{2,1,0:T(8,128)(2,1)S(1)}, bf16[1,144,288]{2,1,0:T(8,128)(2,1)S(1)}, u32[]{:S(2)}, u32[]{:S(2)}) collective-permute-start(bf16[1,144,288]{2,1,0:T(8,128)(2,1)S(1)} %slice.316), channel_id=1, source_target_pairs={{0,16},{1,17},{2,18},{3,19},{4,20},{5,21},{6,22},{7,23},{8,24},{9,... | collective-permute-start | bytes 248840 | tf_op jit(solution)/shard_map/ppermute | solution.py:222
  1511.6 21.5 %collective-permute-start.34 = (bf16[2,144,1076]{2,1,0:T(8,128)(2,1)S(1)}, bf16[2,144,1076]{2,1,0:T(8,128)(2,1)S(1)}, u32[]{:S(2)}, u32[]{:S(2)}) collective-permute-start(bf16[2,144,1076]{2,1,0:T(8,128)(2,1)S(1)} %slice.322), channel_id=1, source_target_pairs={{0,8},{1,9},{2,10},{3,11},{4,12},{5,13},{6,14},{7,15},{8,0},{9,1},... | collective-permute-start | bytes 1859336 | tf_op jit(solution)/shard_map/ppermute | solution.py:222
  1513.8 35.0 %collective-permute-start.38 = (bf16[2,144,1076]{2,1,0:T(8,128)(2,1)S(1)}, bf16[2,144,1076]{2,1,0:T(8,128)(2,1)S(1)}, u32[]{:S(2)}, u32[]{:S(2)}) collective-permute-start(bf16[2,144,1076]{2,1,0:T(8,128)(2,1)S(1)} %slice.330), channel_id=1, source_target_pairs={{0,8},{1,9},{2,10},{3,11},{4,12},{5,13},{6,14},{7,15},{8,0},{9,1},... | collective-permute-start | bytes 1859336 | tf_op jit(solution)/shard_map/ppermute | solution.py:222
  1517.7 31.4 %collective-permute-start.25 = (bf16[4,144,864]{2,1,0:T(8,128)(2,1)S(1)}, bf16[4,144,864]{2,1,0:T(8,128)(2,1)S(1)}, u32[]{:S(2)}, u32[]{:S(2)}) collective-permute-start(bf16[4,144,864]{2,1,0:T(8,128)(2,1)S(1)} %slice.297), channel_id=1, source_target_pairs={{0,4},{1,3},{2,6},{3,1},{4,0},{5,7},{6,2},{7,5},{8,12},{9,11},{10,... | collective-permute-start | bytes 2985992 | tf_op jit(solution)/shard_map/ppermute | solution.py:222
  1549.0 19.9 %collective-permute-start.39 = (bf16[1,144,1076]{2,1,0:T(8,128)(2,1)S(1)}, bf16[1,144,1076]{2,1,0:T(8,128)(2,1)S(1)}, u32[]{:S(2)}, u32[]{:S(2)}) collective-permute-start(bf16[1,144,1076]{2,1,0:T(8,128)(2,1)S(1)} %slice.332), channel_id=1, source_target_pairs={{0,16},{1,17},{2,18},{3,19},{4,20},{5,21},{6,22},{7,23},{8,24},{9,... | collective-permute-start | bytes 929672 | tf_op jit(solution)/shard_map/ppermute | solution.py:222
  (86 other events, 1677.5 us)

commit v2 on v1

--- a/solution.py
+++ b/solution.py
@@ -36,35 +36,27 @@
     return jax.nn.gelu(values, approximate=True)
 
 
-def attend_forward_body(heads, block, qkv_ref, mixed_ref, lse_ref, q_s, k_s, vt_s, ot_s):
+def attend_forward_body(heads, qkv_ref, mixed_ref, lse_ref):
     cols = heads * HD
     for h in range(heads):
         lo = h * HD
-        q_s[...] = qkv_ref[:, lo : lo + HD]
-        k_s[...] = qkv_ref[:, cols + lo : cols + lo + HD]
-        vt_s[...] = qkv_ref[:, 2 * cols + lo : 2 * cols + lo + HD].T
-
-        def one_block(j, carry):
-            at = pl.ds(pl.multiple_of(j * block, block), block)
-            scores = dot(k_s[...], q_s[at, :], NT)
-            highest = jnp.max(scores, axis=0, keepdims=True)
-            probs = jnp.exp2((scores - highest) * SCALE_LOG2)
-            total = jnp.sum(probs, axis=0, keepdims=True)
-            mixed = dot(vt_s[...], probs.astype(LOW))
-            ot_s[:, at] = mixed / total
-            lse_ref[h : h + 1, at] = highest * SCALE_LOG2 + jnp.log2(total)
-            return carry
-
-        lax.fori_loop(0, LEN // block, one_block, 0)
-        mixed_ref[:, lo : lo + HD] = ot_s[...].T.astype(LOW)
+        queries = qkv_ref[:, lo : lo + HD]
+        keys = qkv_ref[:, cols + lo : cols + lo + HD]
+        values = qkv_ref[:, 2 * cols + lo : 2 * cols + lo + HD]
+        scores = dot(keys, queries, NT)
+        highest = jnp.max(scores, axis=0, keepdims=True)
+        probs = jnp.exp2((scores - highest) * SCALE_LOG2)
+        total = jnp.sum(probs, axis=0, keepdims=True)
+        mixed = dot(values.T, probs.astype(LOW)) / total
+        lse_ref[h : h + 1, :] = highest * SCALE_LOG2 + jnp.log2(total)
+        mixed_ref[:, lo : lo + HD] = mixed.T.astype(LOW)
 
 
 def attend_forward(qkv, heads):
     images, rows, _ = qkv.shape
     cols = heads * HD
-    block = 256
     return pl.pallas_call(
-        functools.partial(attend_forward_body, heads, block),
+        functools.partial(attend_forward_body, heads),
         grid=(images,),
         in_specs=[pl.BlockSpec((None, rows, 3 * cols), lambda i: (i, 0, 0))],
         out_specs=[
@@ -75,15 +67,9 @@
             jax.ShapeDtypeStruct((images, rows, cols), LOW),
             jax.ShapeDtypeStruct((images, heads, rows), F32),
         ],
-        scratch_shapes=[
-            pltpu.VMEM((rows, HD), LOW),
-            pltpu.VMEM((rows, HD), LOW),
-            pltpu.VMEM((HD, rows), LOW),
-            pltpu.VMEM((HD, rows), F32),
-        ],
         compiler_params=pltpu.CompilerParams(vmem_limit_bytes=VMEM_LIMIT),
         cost_estimate=pl.CostEstimate(
-            flops=images * heads * rows * rows * 1024,
+            flops=images * heads * rows * rows * 2048,
             bytes_accessed=images * rows * cols * 8,
             transcendentals=images * heads * rows * rows,
         ),
@@ -91,49 +77,29 @@
     )(qkv)
 
 
-def attend_backward_body(
-    heads, block, qkv_ref, grad_ref, mixed_ref, lse_ref, out_ref, q_s, k_s, v_s, do_s, kt_s, dqt_s, dk_s, dv_s, delta_s
-):
+def attend_backward_body(heads, qkv_ref, grad_ref, mixed_ref, lse_ref, out_ref):
     cols = heads * HD
     for h in range(heads):
         lo = h * HD
-        q_s[...] = qkv_ref[:, lo : lo + HD]
+        queries = qkv_ref[:, lo : lo + HD]
         keys = qkv_ref[:, cols + lo : cols + lo + HD]
-        k_s[...] = keys
-        kt_s[...] = keys.T
-        v_s[...] = qkv_ref[:, 2 * cols + lo : 2 * cols + lo + HD]
+        values = qkv_ref[:, 2 * cols + lo : 2 * cols + lo + HD]
         grads = grad_ref[:, lo : lo + HD]
-        do_s[...] = grads
         products = grads.astype(F32) * mixed_ref[:, lo : lo + HD].astype(F32)
-        delta_s[...] = jnp.sum(products.T, axis=0, keepdims=True)
-        dk_s[...] = jnp.zeros_like(dk_s)
-        dv_s[...] = jnp.zeros_like(dv_s)
-
-        def one_block(j, carry):
-            at = pl.ds(pl.multiple_of(j * block, block), block)
-            query = q_s[at, :]
-            grad = do_s[at, :]
-            scores = dot(k_s[...], query, NT)
-            probs = jnp.exp2(scores * SCALE_LOG2 - lse_ref[h : h + 1, at])
-            prob_grad = dot(v_s[...], grad, NT)
-            dv_s[...] += dot(probs.astype(LOW), grad)
-            score_grad = (probs * (prob_grad - delta_s[:, at])).astype(LOW)
-            dk_s[...] += dot(score_grad, query)
-            dqt_s[:, at] = dot(kt_s[...], score_grad)
-            return carry
-
-        lax.fori_loop(0, LEN // block, one_block, 0)
-        out_ref[:, lo : lo + HD] = (dqt_s[...] * SCALE).T.astype(LOW)
-        out_ref[:, cols + lo : cols + lo + HD] = (dk_s[...] * SCALE).astype(LOW)
-        out_ref[:, 2 * cols + lo : 2 * cols + lo + HD] = dv_s[...].astype(LOW)
+        delta = jnp.sum(products.T, axis=0, keepdims=True)
+        probs = jnp.exp2(dot(keys, queries, NT) * SCALE_LOG2 - lse_ref[h : h + 1, :])
+        prob_grad = dot(values, grads, NT)
+        out_ref[:, 2 * cols + lo : 2 * cols + lo + HD] = dot(probs.astype(LOW), grads).astype(LOW)
+        score_grad = (probs * (prob_grad - delta)).astype(LOW)
+        out_ref[:, cols + lo : cols + lo + HD] = (dot(score_grad, queries) * SCALE).astype(LOW)
+        out_ref[:, lo : lo + HD] = (dot(keys.T, score_grad) * SCALE).T.astype(LOW)
 
 
 def attend_backward(qkv, grads, mixed, lse, heads):
     images, rows, _ = qkv.shape
     cols = heads * HD
-    block = 256
     return pl.pallas_call(
-        functools.partial(attend_backward_body, heads, block),
+        functools.partial(attend_backward_body, heads),
         grid=(images,),
         in_specs=[
             pl.BlockSpec((None, rows, 3 * cols), lambda i: (i, 0, 0)),
@@ -143,20 +109,9 @@
         ],
         out_specs=pl.BlockSpec((None, rows, 3 * cols), lambda i: (i, 0, 0)),
         out_shape=jax.ShapeDtypeStruct((images, rows, 3 * cols), LOW),
-        scratch_shapes=[
-            pltpu.VMEM((rows, HD), LOW),
-            pltpu.VMEM((rows, HD), LOW),
-            pltpu.VMEM((rows, HD), LOW),
-            pltpu.VMEM((rows, HD), LOW),
-            pltpu.VMEM((HD, rows), LOW),
-            pltpu.VMEM((HD, rows), F32),
-            pltpu.VMEM((rows, HD), F32),
-            pltpu.VMEM((rows, HD), F32),
-            pltpu.VMEM((1, rows), F32),
-        ],
         compiler_params=pltpu.CompilerParams(vmem_limit_bytes=VMEM_LIMIT),
         cost_estimate=pl.CostEstimate(
-            flops=images * heads * rows * rows * 2560,
+            flops=images * heads * rows * rows * 4096,
             bytes_accessed=images * rows * cols * 18,
             transcendentals=images * heads * rows * rows,
         ),
@@ -189,14 +144,79 @@
     count = table.shape[0]
     if shape[0] % 16:
         return jnp.take(jnp.concatenate(sources, axis=0), table, axis=0)
+    size = count * shape[0] * shape[1]
     return pl.pallas_call(
         functools.partial(place_body, count, first),
         in_specs=[pl.BlockSpec(memory_space=pltpu.SMEM)] + [pl.BlockSpec(memory_space=pl.ANY)] * len(sources),
-        out_specs=pl.BlockSpec(memory_space=pl.ANY),
+        out_specs=pl.BlockSpec(memory_space=pltpu.VMEM),
         out_shape=jax.ShapeDtypeStruct((count, *shape), LOW),
         scratch_shapes=[pltpu.SemaphoreType.DMA((count,))],
+        compiler_params=pltpu.CompilerParams(vmem_limit_bytes=VMEM_LIMIT),
+        cost_estimate=pl.CostEstimate(flops=0, bytes_accessed=4 * size, transcendentals=0),
         name=name,
     )(table, *sources)
+
+
+def weight_grad_body(images, n_dp, half, table_ref, left_ref, *refs):
+    rights, (keep_ref, send_ref, turned, product, sem) = refs[:images], refs[images:]
+    width = turned.shape[0]
+    shard_rows = width // n_dp
+    turned[...] = left_ref[...].T
+    step = width // 2
+
+    def piece(start, n):
+        slot = table_ref[n]
+        source = product.at[n // n_dp, pl.ds((n % n_dp) * shard_rows, shard_rows)]
+        for out_ref, mine, index in ((keep_ref, slot < half, slot), (send_ref, slot >= half, slot - half)):
+            @pl.when(mine)
+            def _():
+                copy = pltpu.make_async_copy(source, out_ref.at[index], sem.at[n])
+                if start:
+                    copy.start()
+                else:
+                    copy.wait()
+
+    for i in range(images):
+        for part in range(2):
+            at = pl.ds(part * step, step)
+            product[i, at, :] = dot(turned[at, :], rights[i][...]).astype(LOW)
+            for d in range(part * n_dp // 2, (part + 1) * n_dp // 2):
+                piece(True, i * n_dp + d)
+    for n in range(images * n_dp):
+        piece(False, n)
+
+
+def weight_grad(table, left, rights, n_dp, name):
+    images = len(rights)
+    rows, width = left.shape
+    cols = rights[0].shape[1]
+    shard_rows = width // n_dp
+    half = images * n_dp // 2
+    if shard_rows % 16:
+        whole = jnp.concatenate([dot(left, right, TN).astype(LOW) for right in rights], axis=0)
+        slots = whole.reshape(images * n_dp, shard_rows, cols)
+        order = jnp.zeros_like(table).at[table].set(jnp.arange(table.shape[0], dtype=jnp.int32))
+        slots = jnp.take(slots, order, axis=0)
+        return slots[:half], slots[half:]
+    shape = jax.ShapeDtypeStruct((half, shard_rows, cols), LOW)
+    return pl.pallas_call(
+        functools.partial(weight_grad_body, images, n_dp, half),
+        in_specs=[pl.BlockSpec(memory_space=pltpu.SMEM)] + [pl.BlockSpec(memory_space=pltpu.VMEM)] * (1 + images),
+        out_specs=[pl.BlockSpec(memory_space=pl.ANY)] * 2,
+        out_shape=[shape, shape],
+        scratch_shapes=[
+            pltpu.VMEM((width, rows), LOW),
+            pltpu.VMEM((images, width, cols), LOW),
+            pltpu.SemaphoreType.DMA((images * n_dp,)),
+        ],
+        compiler_params=pltpu.CompilerParams(vmem_limit_bytes=VMEM_LIMIT),
+        cost_estimate=pl.CostEstimate(
+            flops=2 * images * rows * width * cols,
+            bytes_accessed=2 * (rows * width + images * (rows + width) * cols),
+            transcendentals=0,
+        ),
+        name=name,
+    )(table, left, *rights)
 
 
 class Plan:
@@ -254,13 +274,14 @@
             mine = jnp.concatenate([mine, theirs], axis=0)
         return (mine,)
 
-    def scatter(self, pieces):
+    def scatter(self, keep, send):
         for stage in reversed(range(self.stages)):
-            half = pieces.shape[0] // 2
-            theirs = self.exchange(pieces[half:], stage)
-            total = pieces[:half].astype(F32) + theirs.astype(F32)
-            pieces = total if stage == 0 else total.astype(LOW)
-        return pieces[0]
+            theirs = self.exchange(send, stage)
+            half = keep.shape[0] // 2
+            if stage == 0:
+                return (keep.astype(F32) + theirs.astype(F32))[0]
+            send = (keep[half:].astype(F32) + theirs[half:].astype(F32)).astype(LOW)
+            keep = (keep[:half].astype(F32) + theirs[:half].astype(F32)).astype(LOW)
 
     def rank_gather(self, shard):
         mine = shard
@@ -288,7 +309,6 @@
     me_t = lax.axis_index("tensor")
     me_image, me_rank = me_t // ranks, me_t % ranks
     slot_table = plan.slots().reshape(-1)
-    piece_table = jnp.zeros_like(slot_table).at[slot_table].set(jnp.arange(slot_table.shape[0], dtype=jnp.int32))
 
     def shard_of(i):
         return (me_image ^ i) * ranks + me_rank
@@ -307,9 +327,8 @@
         full = place(slot_table, plan.gather(shard), name)
         return full.reshape(images, n_dp * shard_rows, shard.shape[1])
 
-    def scattered(grads, name):
-        pieces = jnp.concatenate(grads, axis=0).reshape(images * n_dp, shard_rows, -1)
-        return plan.scatter(place(piece_table, [pieces], name))
+    def scattered(left, rights, name):
+        return plan.scatter(*weight_grad(slot_table, left, rights, n_dp, name))
 
     low = lambda v: v.astype(LOW)
     qkv_full = gathered(jnp.concatenate([low(w_query), low(w_key), low(w_value)], axis=1), "place_qkv")
@@ -341,16 +360,14 @@
 
     grad_out = cotangent.astype(F32)
     down_bias_grad = jnp.sum(grad_out, axis=0)
-    pre_low, down_grads, up_grads, up_bias_parts = [], [], [], []
+    pre_low, up_bias_parts = [], []
     for i in range(images):
-        down_grads.append(low(dot(cot_rows, act[i], TN)))
         act_grad = dot(cot_rows, down_full[i])
         _, pull = jax.vjp(gelu_tanh, pre_act[i])
         pre_low.append(low(pull(act_grad)[0]))
         up_bias_parts.append(jnp.sum(pre_low[i], axis=0, dtype=F32))
-        up_grads.append(low(dot(rows_two, pre_low[i], TN)))
-    down_grad = scattered(down_grads, "place_grad_down").T
-    up_grad = scattered(up_grads, "place_grad_up")
+    down_grad = scattered(cot_rows, act, "grad_down").T
+    up_grad = scattered(rows_two, pre_low, "grad_up")
     up_bias_grad = uncolumns(jnp.stack(up_bias_parts), b_up.shape[0])
     norm_two_grad = plan.rank_scatter(sum(dot(pre_low[i], up_full[i], NT) for i in range(images)))
     _, pull_two = jax.vjp(layer_norm, residual, gain_two, shift_two)
@@ -361,9 +378,9 @@
     branch_rows = plan.rank_gather(branch_low)
 
     mixed_grad = jnp.stack([low(dot(branch_rows, out_full[i])) for i in range(images)])
-    out_grad = scattered([low(dot(branch_rows, mixed[i], TN)) for i in range(images)], "place_grad_out").T
+    out_grad = scattered(branch_rows, list(mixed), "grad_out").T
     qkv_grads = attend_backward(qkv, mixed_grad, mixed, lse, heads)
-    qkv_grad = scattered([low(dot(rows_one, qkv_grads[i], TN)) for i in range(images)], "place_grad_qkv")
+    qkv_grad = scattered(rows_one, list(qkv_grads), "grad_qkv")
     query_grad, key_grad, value_grad = (qkv_grad[:, n * head_cols : (n + 1) * head_cols] for n in range(3))
     qkv_sums = jnp.sum(qkv_grads, axis=1, dtype=F32)
     query_bias_grad = uncolumns(qkv_sums[:, :head_cols], b_query.shape[0])

time: 1590 us -> 541 us (0.34)
  Pallas kernels: 1090 us -> 97.3 us
  local copies, waits for them, and re-layouts: 70.3 us -> 23.8 us
  matrix products: 103 us -> 73.1 us
  waiting for transfers between devices: 158 us -> 179 us
    pallas_call x8 -> x4, Pallas kernels: 1020 us -> 21.6 us  [place(): pl.pallas_call(functools.partial(place_body, count, first), in_specs=[pl....]
    dot_general x24 -> x16, matrix products: 103 us -> 73.1 us  [dot(): return lax.dot_general(left, right, dims, preferred_element_type=F32)]
    concatenate x4 -> x0, local copies, waits for them, and re-layouts: 26.3 us -> none  [scattered(): jnp.concatenate(grads, axis=0).reshape(images * n_dp, shard_rows, -1)]
    ppermute x40, waiting for transfers between devices: 158 us -> 179 us  [permute(): return lax.ppermute(values, ('dp', 'tensor'), pairs)]
    pallas_call x2 -> x6, Pallas kernels: 72 us -> 75.6 us  [the longest x4 35.1 us: weight_grad(): pl.pallas_call(functools.partial(weight_grad_body, images, n_dp, half), i...]
  transfers between devices with their start and end apart: 40 -> 40, of which waited for: 13 -> 14; matrix products, arithmetic and copies ran while one was open for 12% -> 21% of each run, Pallas kernels for 69% -> 18%
where the time goes in v2:
time: 541 us; the launch traced here: 532 us
  waiting for transfers between devices  179 us (33%)
  Pallas kernels  97.3 us (18%)
  matrix products  73.1 us (14%)
  other arithmetic  65.1 us (12%)
  blocking collectives  53.3 us (10%)
  starting transfers between devices  39 us (7%)
  local copies, waits for them, and re-layouts  23.8 us (4%)
    ppermute x40, waiting for transfers between devices, permute(): return lax.ppermute(values, ('dp', 'tensor'), pairs)  179 us
    dot_general x16, matrix products, dot(): return lax.dot_general(left, right, dims, preferred_element_type=F32)  73.1 us
    psum x1, blocking collectives, local(): lax.psum((gain_one_grad, shift_one_grad, query_bias_grad, value_bias_grad...  53.3 us
    ppermute x40, starting transfers between devices, permute(): return lax.ppermute(values, ('dp', 'tensor'), pairs)  39 us
    pallas_call x4, Pallas kernels, weight_grad(): pl.pallas_call(functools.partial(weight_grad_body, images, n_dp, half), i...  35.1 us
    pallas_call x1, Pallas kernels, attend_backward(): pl.pallas_call(functools.partial(attend_backward_body, heads), grid=(imag...  24.9 us
    pallas_call x4, Pallas kernels, place(): pl.pallas_call(functools.partial(place_body, count, first), in_specs=[pl....  21.6 us
    concatenate x12, other arithmetic, gather(): mine = jnp.concatenate([mine, theirs], axis=0)  17.4 us
  transfers between devices with their start and end apart: 40, of which 14 were waited for; matrix products, arithmetic and copies ran while one was open for 21% of the time, Pallas kernels for 18%

profile of v2, /device:TPU:0, one launch (start us, length us, event | category | flops | bytes accessed | tf_op | source)
XLA Modules:
  0.0 532.4 jit_solution(452517572828329622)
XLA Ops:
  3.9 4.1 collective-permute-start.1
  14.7 22.6 %collective-permute-done.1 = bf16[1,144,864]{2,1,0:T(8,128)(2,1)} collective-permute-done((bf16[1,144,864]{2,1,0:T(8,128)(2,1)S(1)}, bf16[1,144,864]{2,1,0:T(8,128)(2,1)}, u32[]{:S(2)}, u32[]{:S(2)}) %collective-permute-start.1) | collective-permute-done | bytes 248864 | tf_op jit(solution)/shard_map/ppermute | solution.py:242
  38.7 8.2 %collective-permute-done.15 = bf16[1,144,1076]{2,1,0:T(8,128)(2,1)} collective-permute-done((bf16[1,144,1076]{2,1,0:T(8,128)(2,1)S(1)}, bf16[1,144,1076]{2,1,0:T(8,128)(2,1)}, u32[]{:S(2)}, u32[]{:S(2)}) %collective-permute-start.15) | collective-permute-done | bytes 309920 | tf_op jit(solution)/shard_map/ppermute | solution.py:242
  48.8 15.3 %collective-permute-done.2 = bf16[2,144,864]{2,1,0:T(8,128)(2,1)S(1)} collective-permute-done((bf16[2,144,864]{2,1,0:T(8,128)(2,1)S(1)}, bf16[2,144,864]{2,1,0:T(8,128)(2,1)S(1)}, u32[]{:S(2)}, u32[]{:S(2)}) %collective-permute-start.2) | collective-permute-done | bytes 497696 | tf_op jit(solution)/shard_map/ppermute | solution.py:242
  72.9 10.2 %collective-permute-done.6 = bf16[2,144,288]{2,1,0:T(8,128)(2,1)S(1)} collective-permute-done((bf16[2,144,288]{2,1,0:T(8,128)(2,1)S(1)}, bf16[2,144,288]{2,1,0:T(8,128)(2,1)S(1)}, u32[]{:S(2)}, u32[]{:S(2)}) %collective-permute-start.6) | collective-permute-done | bytes 165920 | tf_op jit(solution)/shard_map/ppermute | solution.py:242
  103.2 48.2 %collective-permute-done.8.refs_1_ = bf16[8,144,288]{2,1,0:T(8,128)(2,1)S(1)} collective-permute-done((bf16[8,144,288]{2,1,0:T(8,128)(2,1)S(1)}, bf16[8,144,288]{2,1,0:T(8,128)(2,1)S(1)}, u32[]{:S(2)}, u32[]{:S(2)}) %collective-permute-start.8) | collective-permute-done | bytes 663584 | tf_op jit(solution)/shard_map/ppermute | solution.py:242
  161.2 7.0 %place_qkv.1 = bf16[16,144,864]{2,1,0:T(8,128)(2,1)} custom-call(s32[16]{0:T(128)S(1)} %select_n.106.table_ref, bf16[8,144,864]{2,1,0:T(8,128)(2,1)S(1)} %pad_maximum_fusion.6.refs_0_, bf16[8,144,864]{2,1,0:T(8,128)(2,1)} %collective-permute-done.4.refs_1_), custom_call_target="tpu_custom_call" | custom-call | bytes 7962624 | tf_op jit(solution)/shard_map/place_qkv/pallas_call | solution.py:148
  170.8 5.9 %fusion.29 = bf16[1,1024,864]{2,1,0:T(8,128)(2,1)S(1)} fusion(f32[864]{0:T(1024)S(1)} %get-tuple-element.47, bf16[1152,864]{1,0:T(8,128)(2,1)S(1)} %bitcast.92, bf16[512,1152]{1,0:T(8,128)(2,1)} %collective-permute-done, bf16[512,1152]{1,0:T(8,128)(2,1)} %fusion.21), kind=kOutput, calls=%fused_computation.80 | convolution fusion | flops 2044919808 | bytes 6122880 | tf_op jit(solution)/shard_map/dot_general | solution.py:26
  176.7 4.4 fusion.30
  183.5 15.6 %attend_forward.1 = (bf16[2,1024,288]{2,1,0:T(8,128)(2,1)S(1)}, f32[2,4,1024]{2,1,0:T(4,128)S(1)}) custom-call(bf16[2,1024,864]{2,1,0:T(8,128)(2,1)} %pad_maximum_fusion.qkv_ref), custom_call_target="tpu_custom_call" | custom-call | flops 17179869184 | bytes 4718592 | tf_op jit(solution)/shard_map/attend_forward/pallas_call | solution.py:58
  204.5 5.6 %place_down.1 = bf16[16,144,1076]{2,1,0:T(8,128)(2,1)} custom-call(s32[16]{0:T(128)S(1)} %select_n.106.table_ref, bf16[8,144,1076]{2,1,0:T(8,128)(2,1)S(1)} %pad_maximum_fusion.2.refs_0_, bf16[8,144,1076]{2,1,0:T(8,128)(2,1)} %collective-permute-done.18.refs_1_), custom_call_target="tpu_custom_call" | custom-call | bytes 9916416 | tf_op jit(solution)/shard_map/place_down/pallas_call | solution.py:148
  210.1 8.0 %collective-permute-done.14.refs_1_ = bf16[8,144,1076]{2,1,0:T(8,128)(2,1)} collective-permute-done((bf16[8,144,1076]{2,1,0:T(8,128)(2,1)S(1)}, bf16[8,144,1076]{2,1,0:T(8,128)(2,1)}, u32[]{:S(2)}, u32[]{:S(2)}) %collective-permute-start.14) | collective-permute-done | bytes 2479136 | tf_op jit(solution)/shard_map/ppermute | solution.py:242
  218.0 5.8 %place_up.1 = bf16[16,144,1076]{2,1,0:T(8,128)(2,1)} custom-call(s32[16]{0:T(128)S(1)} %select_n.106.table_ref, bf16[8,144,1076]{2,1,0:T(8,128)(2,1)S(1)} %pad_maximum_fusion.1.refs_0_, bf16[8,144,1076]{2,1,0:T(8,128)(2,1)} %collective-permute-done.14.refs_1_), custom_call_target="tpu_custom_call" | custom-call | bytes 9916416 | tf_op jit(solution)/shard_map/place_up/pallas_call | solution.py:148
  227.0 5.3 fusion.59
  238.2 7.4 %convert_reduce_fusion.1 = (f32[1076]{0:T(1024)S(1)}, bf16[1024,1076]{1,0:T(8,128)(2,1)S(1)}, bf16[1024,1076]{1,0:T(8,128)(2,1)S(1)}) fusion(f32[1024,1076]{1,0:T(8,128)S(1)} %fusion.60, f32[1076]{0:T(1024)S(1)} %get-tuple-element.107, bf16[1152,1076]{1,0:T(8,128)(2,1)S(1)} %bitcast.90, bf16[512,1152]{1,0:T(8,128)(2,1)S(1)} %collective-permute-done.10, ...), kind=kOutput, calls=%fused_computation.20 | convolution fusion | flops 2570865664 | bytes 13661600 | tf_op jit(solution)/shard_map/dot_general | solution.py:26
  245.6 5.2 fusion.58
  254.5 9.3 %convert_reduce_fusion.2 = (f32[1076]{0:T(1024)S(1)}, bf16[1024,1076]{1,0:T(8,128)(2,1)}, bf16[1024,1076]{1,0:T(8,128)(2,1)}) fusion(f32[1024,1076]{1,0:T(8,128)S(1)} %bitcast.97, f32[1076]{0:T(1024)S(1)} %get-tuple-element.106, bf16[1152,1076]{1,0:T(8,128)(2,1)S(1)} %bitcast.88, bf16[512,1152]{1,0:T(8,128)(2,1)S(1)} %collective-permute-done.10, ...), kind=kOutput, calls=%fused_computation.21 | convolution fusion | flops 2570865664 | bytes 13661600 | tf_op jit(solution)/shard_map/dot_general | solution.py:26
  263.9 5.5 %convolution_add_fusion.2 = f32[1024,1152]{1,0:T(8,128)S(1)} fusion(f32[1024,1152]{1,0:T(8,128)S(1)} %fusion.61, bf16[1024,1076]{1,0:T(8,128)(2,1)} %get-tuple-element.61.refs_0_, bf16[1152,1076]{1,0:T(8,128)(2,1)S(1)} %bitcast.89), kind=kOutput, calls=%fused_computation.25 | convolution fusion | flops 2539782144 | bytes 14119936 | tf_op jit(solution)/shard_map/dot_general | solution.py:26
  285.1 10.1 %grad_down.1 = (bf16[8,144,1076]{2,1,0:T(8,128)(2,1)}, bf16[8,144,1076]{2,1,0:T(8,128)(2,1)}) custom-call(s32[16]{0:T(128)S(1)} %select_n.106.table_ref, bf16[1024,1152]{1,0:T(8,128)(2,1)S(1)} %copy-done.2, bf16[1024,1076]{1,0:T(8,128)(2,1)} %get-tuple-element.78.refs_0_, bf16[1024,1076]{1,0:T(8,128)(2,1)} %copy-done.50), custom_call_target="tpu_custom_call" | custom-call | flops 5077204992 | bytes 11724800 | tf_op jit(solution)/shard_map/grad_down/pallas_call | solution.py:202
  297.1 10.0 %grad_up.1 = (bf16[8,144,1076]{2,1,0:T(8,128)(2,1)}, bf16[8,144,1076]{2,1,0:T(8,128)(2,1)}) custom-call(s32[16]{0:T(128)S(1)} %select_n.106.table_ref, bf16[1024,1152]{1,0:T(8,128)(2,1)S(1)} %pad_maximum_fusion.4.left_ref, bf16[1024,1076]{1,0:T(8,128)(2,1)} %get-tuple-element.61.refs_0_, bf16[1024,1076]{1,0:T(8,128)(2,1)} %copy-done.49), custom_call_target="tpu_custom_call" | custom-call | flops 5077204992 | bytes 11724800 | tf_op jit(solution)/shard_map/grad_up/pallas_call | solution.py:202
  311.4 7.0 %grad_out.1 = (bf16[8,144,288]{2,1,0:T(8,128)(2,1)S(1)}, bf16[8,144,288]{2,1,0:T(8,128)(2,1)}) custom-call(s32[16]{0:T(128)S(1)} %select_n.106.table_ref, bf16[1024,1152]{1,0:T(8,128)(2,1)} %pad_maximum_fusion.5.left_ref, bf16[1024,288]{1,0:T(8,128)(2,1)S(1)} %copy-done, bf16[1024,288]{1,0:T(8,128)(2,1)S(1)} %get-tuple-element.97.refs_1_), custom_call_target="tpu_custom_call" | custom-call | flops 1358954496 | bytes 4866048 | tf_op jit(solution)/shard_map/grad_out/pallas_call | solution.py:202
  326.6 24.9 %attend_backward.1 = bf16[2,1024,864]{2,1,0:T(8,128)(2,1)} custom-call(bf16[2,1024,864]{2,1,0:T(8,128)(2,1)} %pad_maximum_fusion.qkv_ref, bf16[2,1024,288]{2,1,0:T(8,128)(2,1)S(1)} %pad_maximum_fusion.7.grad_ref, bf16[2,1024,288]{2,1,0:T(8,128)(2,1)S(1)} %get-tuple-element.27.mixed_ref, f32[2,4,1024]{2,1,0:T(4,128)S(1)} %get-tuple-element.28.lse_ref), custom_call_target="tpu_custom_call" | custom-call | flops 34359738368 | bytes 10616832 | tf_op jit(solution)/shard_map/attend_backward/pallas_call | solution.py:101
  355.3 4.7 fusion.40
  360.1 7.9 %grad_qkv.1 = (bf16[8,144,864]{2,1,0:T(8,128)(2,1)}, bf16[8,144,864]{2,1,0:T(8,128)(2,1)}) custom-call(s32[16]{0:T(128)S(1)} %select_n.106.table_ref, bf16[1024,1152]{1,0:T(8,128)(2,1)} %pad_maximum_fusion.3.left_ref, bf16[1024,864]{1,0:T(8,128)(2,1)S(1)} %get-tuple-element.85.refs_0_, bf16[1024,864]{1,0:T(8,128)(2,1)S(1)} %get-tuple-element.84.refs_1_), custom_call_target="tpu_custom_call" | custom-call | flops 4076863488 | bytes 9879552 | tf_op jit(solution)/shard_map/grad_qkv/pallas_call | solution.py:202
  368.5 5.4 %convolution_add_fusion.1 = f32[1024,1152]{1,0:T(8,128)S(1)} fusion(f32[1024,1152]{1,0:T(8,128)} %fusion.40, bf16[1152,864]{1,0:T(8,128)(2,1)} %bitcast.93, bf16[2,1024,864]{2,1,0:T(8,128)(2,1)S(1)} %copy-done.7), kind=kOutput, calls=%fused_computation.24 | convolution fusion | flops 2039611392 | bytes 13262848 | tf_op jit(solution)/shard_map/dot_general | solution.py:26
  380.6 4.4 add_convert_fusion.3
  385.5 6.7 %collective-permute-done.29 = bf16[4,144,288]{2,1,0:T(8,128)(2,1)S(1)} collective-permute-done((bf16[4,144,288]{2,1,0:T(8,128)(2,1)S(1)}, bf16[4,144,288]{2,1,0:T(8,128)(2,1)S(1)}, u32[]{:S(2)}, u32[]{:S(2)}) %collective-permute-start.29) | collective-permute-done | bytes 331808 | tf_op jit(solution)/shard_map/ppermute | solution.py:242
  408.0 53.3 %all-reduce = (f32[1152]{0:T(1024)}, f32[1152]{0:T(1024)}, f32[1152]{0:T(1024)}, f32[1152]{0:T(1024)}, f32[1152]{0:T(1024)}, /*index=5*/f32[1152]{0:T(1024)}, f32[1152]{0:T(1024)}, f32[4304]{0:T(1024)}, f32[1152]{0:T(1024)}) all-reduce(f32[1152]{0:T(1024)S(1)} %get-tuple-element.39, ...), channel_id=1, replica_groups=mesh['dp'=8,'tensor'=4] {'dp','tensor'}, use_global_device_ids=true, to_apply=%region_9.10 | all-reduce | flops 13520 | bytes 108160 | tf_op jit(solution)/shard_map/psum | solution.py:393
  471.6 12.9 %collective-permute-done.38 = bf16[2,144,1076]{2,1,0:T(8,128)(2,1)S(1)} collective-permute-done((bf16[2,144,1076]{2,1,0:T(8,128)(2,1)S(1)}, bf16[2,144,1076]{2,1,0:T(8,128)(2,1)S(1)}, u32[]{:S(2)}, u32[]{:S(2)}) %collective-permute-start.38) | collective-permute-done | bytes 619808 | tf_op jit(solution)/shard_map/ppermute | solution.py:242
  484.6 15.6 %collective-permute-done.34 = bf16[2,144,1076]{2,1,0:T(8,128)(2,1)S(1)} collective-permute-done((bf16[2,144,1076]{2,1,0:T(8,128)(2,1)S(1)}, bf16[2,144,1076]{2,1,0:T(8,128)(2,1)S(1)}, u32[]{:S(2)}, u32[]{:S(2)}) %collective-permute-start.34) | collective-permute-done | bytes 619808 | tf_op jit(solution)/shard_map/ppermute | solution.py:242
  503.8 15.8 %collective-permute-done.26 = bf16[2,144,864]{2,1,0:T(8,128)(2,1)S(1)} collective-permute-done((bf16[2,144,864]{2,1,0:T(8,128)(2,1)S(1)}, bf16[2,144,864]{2,1,0:T(8,128)(2,1)S(1)}, u32[]{:S(2)}, u32[]{:S(2)}) %collective-permute-start.26) | collective-permute-done | bytes 497696 | tf_op jit(solution)/shard_map/ppermute | solution.py:242
  521.0 10.1 %collective-permute-done.27 = bf16[1,144,864]{2,1,0:T(8,128)(2,1)S(1)} collective-permute-done((bf16[1,144,864]{2,1,0:T(8,128)(2,1)S(1)}, bf16[1,144,864]{2,1,0:T(8,128)(2,1)S(1)}, u32[]{:S(2)}, u32[]{:S(2)}) %collective-permute-start.27) | collective-permute-done | bytes 248864 | tf_op jit(solution)/shard_map/ppermute | solution.py:242
  (298 shorter events, 147.7 us)
Async XLA Ops:
  3.9 33.4 %collective-permute-start.1 = (bf16[1,144,864]{2,1,0:T(8,128)(2,1)S(1)}, bf16[1,144,864]{2,1,0:T(8,128)(2,1)}, u32[]{:S(2)}, u32[]{:S(2)}) collective-permute-start(bf16[1,144,864]{2,1,0:T(8,128)(2,1)S(1)} %maximum_bitcast_fusion), channel_id=1, source_target_pairs={{0,16},{1,17},{2,18},{3,19},{4,20},{5,21},{6,22},{7,23},{8,24},{9,... | collective-permute-start | bytes 746504 | tf_op jit(solution)/shard_map/ppermute | solution.py:242
  9.0 59.7 %collective-permute-start.5 = (bf16[1,144,288]{2,1,0:T(8,128)(2,1)S(1)}, bf16[1,144,288]{2,1,0:T(8,128)(2,1)}, u32[]{:S(2)}, u32[]{:S(2)}) collective-permute-start(bf16[1,144,288]{2,1,0:T(8,128)(2,1)S(1)} %convert_bitcast_fusion.2), channel_id=1, source_target_pairs={{0,16},{1,17},{2,18},{3,19},{4,20},{5,21},{6,22},{7,23},{8,24},{9,... | collective-permute-start | bytes 248840 | tf_op jit(solution)/shard_map/ppermute | solution.py:242
  9.1 37.8 %collective-permute-start.15 = (bf16[1,144,1076]{2,1,0:T(8,128)(2,1)S(1)}, bf16[1,144,1076]{2,1,0:T(8,128)(2,1)}, u32[]{:S(2)}, u32[]{:S(2)}) collective-permute-start(bf16[1,144,1076]{2,1,0:T(8,128)(2,1)S(1)} %convert_bitcast_fusion), channel_id=1, source_target_pairs={{0,16},{1,17},{2,18},{3,19},{4,20},{5,21},{6,22},{7,23},{8,24},{9,... | collective-permute-start | bytes 929672 | tf_op jit(solution)/shard_map/ppermute | solution.py:242
  12.1 88.2 %collective-permute-start.20 = (bf16[512,1152]{1,0:T(8,128)(2,1)S(1)}, bf16[512,1152]{1,0:T(8,128)(2,1)}, u32[]{:S(2)}, u32[]{:S(2)}) collective-permute-start(bf16[512,1152]{1,0:T(8,128)(2,1)S(1)} %copy-done.9), channel_id=1, source_target_pairs={{0,1},{1,0},{2,3},{3,2},{4,5},{5,4},{6,7},{7,6},{8,9},{9,8},{10,11... | collective-permute-start | bytes 3538952 | tf_op jit(solution)/shard_map/ppermute | solution.py:242
  12.2 57.6 %collective-permute-start.11 = (bf16[1,144,1076]{2,1,0:T(8,128)(2,1)S(1)}, bf16[1,144,1076]{2,1,0:T(8,128)(2,1)}, u32[]{:S(2)}, u32[]{:S(2)}) collective-permute-start(bf16[1,144,1076]{2,1,0:T(8,128)(2,1)S(1)} %convert_bitcast_fusion.1), channel_id=1, source_target_pairs={{0,16},{1,17},{2,18},{3,19},{4,20},{5,21},{6,22},{7,23},{8,24},{9,... | collective-permute-start | bytes 929672 | tf_op jit(solution)/shard_map/ppermute | solution.py:242
  38.3 25.8 %collective-permute-start.2 = (bf16[2,144,864]{2,1,0:T(8,128)(2,1)S(1)}, bf16[2,144,864]{2,1,0:T(8,128)(2,1)S(1)}, u32[]{:S(2)}, u32[]{:S(2)}) collective-permute-start(bf16[2,144,864]{2,1,0:T(8,128)(2,1)S(1)} %pad_maximum_fusion.14), channel_id=1, source_target_pairs={{0,8},{1,9},{2,10},{3,11},{4,12},{5,13},{6,14},{7,15},{8,0},{9,1},... | collective-permute-start | bytes 1493000 | tf_op jit(solution)/shard_map/ppermute | solution.py:242
  48.8 36.9 %collective-permute-start.16 = (bf16[2,144,1076]{2,1,0:T(8,128)(2,1)}, bf16[2,144,1076]{2,1,0:T(8,128)(2,1)}, u32[]{:S(2)}, u32[]{:S(2)}) collective-permute-start(bf16[2,144,1076]{2,1,0:T(8,128)(2,1)} %pad_maximum_fusion.13), channel_id=1, source_target_pairs={{0,8},{1,9},{2,10},{3,11},{4,12},{5,13},{6,14},{7,15},{8,0},{9,1},... | collective-permute-start | bytes 1859336 | tf_op jit(solution)/shard_map/ppermute | solution.py:242
  67.0 20.6 %collective-permute-start.3 = (bf16[4,144,864]{2,1,0:T(8,128)(2,1)}, bf16[4,144,864]{2,1,0:T(8,128)(2,1)}, u32[]{:S(2)}, u32[]{:S(2)}) collective-permute-start(bf16[4,144,864]{2,1,0:T(8,128)(2,1)} %pad_maximum_fusion.10), channel_id=1, source_target_pairs={{0,4},{1,3},{2,6},{3,1},{4,0},{5,7},{6,2},{7,5},{8,12},{9,11},{10,... | collective-permute-start | bytes 2985992 | tf_op jit(solution)/shard_map/ppermute | solution.py:242
  70.9 26.3 %collective-permute-start.12 = (bf16[2,144,1076]{2,1,0:T(8,128)(2,1)S(1)}, bf16[2,144,1076]{2,1,0:T(8,128)(2,1)S(1)}, u32[]{:S(2)}, u32[]{:S(2)}) collective-permute-start(bf16[2,144,1076]{2,1,0:T(8,128)(2,1)S(1)} %pad_maximum_fusion.12), channel_id=1, source_target_pairs={{0,8},{1,9},{2,10},{3,11},{4,12},{5,13},{6,14},{7,15},{8,0},{9,1},... | collective-permute-start | bytes 1859336 | tf_op jit(solution)/shard_map/ppermute | solution.py:242
  87.0 67.9 %collective-permute-start.17 = (bf16[4,144,1076]{2,1,0:T(8,128)(2,1)S(1)}, bf16[4,144,1076]{2,1,0:T(8,128)(2,1)}, u32[]{:S(2)}, u32[]{:S(2)}) collective-permute-start(bf16[4,144,1076]{2,1,0:T(8,128)(2,1)S(1)} %pad_maximum_fusion.9), channel_id=1, source_target_pairs={{0,4},{1,3},{2,6},{3,1},{4,0},{5,7},{6,2},{7,5},{8,12},{9,11},{10,... | collective-permute-start | bytes 3718664 | tf_op jit(solution)/shard_map/ppermute | solution.py:242
  89.2 72.0 %collective-permute-start.4 = (bf16[8,144,864]{2,1,0:T(8,128)(2,1)S(1)}, bf16[8,144,864]{2,1,0:T(8,128)(2,1)}, u32[]{:S(2)}, u32[]{:S(2)}) collective-permute-start(bf16[8,144,864]{2,1,0:T(8,128)(2,1)S(1)} %pad_maximum_fusion.6.refs_0_), channel_id=1, source_target_pairs={{0,2},{1,5},{2,0},{3,7},{4,6},{5,1},{6,4},{7,3},{8,10},{9,13},{10,... | collective-permute-start | bytes 5971976 | tf_op jit(solution)/shard_map/ppermute | solution.py:242
  94.7 56.7 %collective-permute-start.8 = (bf16[8,144,288]{2,1,0:T(8,128)(2,1)S(1)}, bf16[8,144,288]{2,1,0:T(8,128)(2,1)S(1)}, u32[]{:S(2)}, u32[]{:S(2)}) collective-permute-start(bf16[8,144,288]{2,1,0:T(8,128)(2,1)S(1)} %pad_maximum_fusion.11.refs_0_), channel_id=1, source_target_pairs={{0,2},{1,5},{2,0},{3,7},{4,6},{5,1},{6,4},{7,3},{8,10},{9,13},{10,... | collective-permute-start | bytes 1990664 | tf_op jit(solution)/shard_map/ppermute | solution.py:242
  98.6 60.5 %collective-permute-start.13 = (bf16[4,144,1076]{2,1,0:T(8,128)(2,1)S(1)}, bf16[4,144,1076]{2,1,0:T(8,128)(2,1)}, u32[]{:S(2)}, u32[]{:S(2)}) collective-permute-start(bf16[4,144,1076]{2,1,0:T(8,128)(2,1)S(1)} %pad_maximum_fusion.8), channel_id=1, source_target_pairs={{0,4},{1,3},{2,6},{3,1},{4,0},{5,7},{6,2},{7,5},{8,12},{9,11},{10,... | collective-permute-start | bytes 3718664 | tf_op jit(solution)/shard_map/ppermute | solution.py:242
  100.3 70.5 %collective-permute-start = (bf16[512,1152]{1,0:T(8,128)(2,1)}, bf16[512,1152]{1,0:T(8,128)(2,1)}, u32[]{:S(2)}, u32[]{:S(2)}) collective-permute-start(bf16[512,1152]{1,0:T(8,128)(2,1)} %fusion.21), channel_id=1, source_target_pairs={{0,1},{1,0},{2,3},{3,2},{4,5},{5,4},{6,7},{7,6},{8,9},{9,8},{10,11... | collective-permute-start | bytes 3538952 | tf_op jit(solution)/shard_map/ppermute | solution.py:242
  157.4 47.1 %collective-permute-start.18 = (bf16[8,144,1076]{2,1,0:T(8,128)(2,1)S(1)}, bf16[8,144,1076]{2,1,0:T(8,128)(2,1)}, u32[]{:S(2)}, u32[]{:S(2)}) collective-permute-start(bf16[8,144,1076]{2,1,0:T(8,128)(2,1)S(1)} %pad_maximum_fusion.2.refs_0_), channel_id=1, source_target_pairs={{0,2},{1,5},{2,0},{3,7},{4,6},{5,1},{6,4},{7,3},{8,10},{9,13},{10,... | collective-permute-start | bytes 7437320 | tf_op jit(solution)/shard_map/ppermute | solution.py:242
  160.6 57.4 %collective-permute-start.14 = (bf16[8,144,1076]{2,1,0:T(8,128)(2,1)S(1)}, bf16[8,144,1076]{2,1,0:T(8,128)(2,1)}, u32[]{:S(2)}, u32[]{:S(2)}) collective-permute-start(bf16[8,144,1076]{2,1,0:T(8,128)(2,1)S(1)} %pad_maximum_fusion.1.refs_0_), channel_id=1, source_target_pairs={{0,2},{1,5},{2,0},{3,7},{4,6},{5,1},{6,4},{7,3},{8,10},{9,13},{10,... | collective-permute-start | bytes 7437320 | tf_op jit(solution)/shard_map/ppermute | solution.py:242
  204.4 28.0 %collective-permute-start.9 = (bf16[512,1152]{1,0:T(8,128)(2,1)S(1)}, bf16[512,1152]{1,0:T(8,128)(2,1)S(1)}, u32[]{:S(2)}, u32[]{:S(2)}) collective-permute-start(bf16[512,1152]{1,0:T(8,128)(2,1)S(1)} %slice.498), channel_id=1, source_target_pairs={{0,1},{1,0},{2,3},{3,2},{4,5},{5,4},{6,7},{7,6},{8,9},{9,8},{10,11... | collective-permute-start | bytes 3538952 | tf_op jit(solution)/shard_map/ppermute | solution.py:242
  285.1 23.0 %collective-permute-start.22 = (bf16[512,1152]{1,0:T(8,128)(2,1)}, bf16[512,1152]{1,0:T(8,128)(2,1)}, u32[]{:S(2)}, u32[]{:S(2)}) collective-permute-start(bf16[512,1152]{1,0:T(8,128)(2,1)} %get-tuple-element.63), channel_id=1, source_target_pairs={{0,1},{1,0},{2,3},{3,2},{4,5},{5,4},{6,7},{7,6},{8,9},{9,8},{10,11... | collective-permute-start | bytes 3538952 | tf_op jit(solution)/shard_map/ppermute | solution.py:242
  295.2 85.4 %collective-permute-start.36 = (bf16[8,144,1076]{2,1,0:T(8,128)(2,1)}, bf16[8,144,1076]{2,1,0:T(8,128)(2,1)}, u32[]{:S(2)}, u32[]{:S(2)}) collective-permute-start(bf16[8,144,1076]{2,1,0:T(8,128)(2,1)} %get-tuple-element.36), channel_id=1, source_target_pairs={{0,2},{1,5},{2,0},{3,7},{4,6},{5,1},{6,4},{7,3},{8,10},{9,13},{10,... | collective-permute-start | bytes 7437320 | tf_op jit(solution)/shard_map/ppermute | solution.py:242
  307.0 85.3 %collective-permute-start.32 = (bf16[8,144,1076]{2,1,0:T(8,128)(2,1)}, bf16[8,144,1076]{2,1,0:T(8,128)(2,1)}, u32[]{:S(2)}, u32[]{:S(2)}) collective-permute-start(bf16[8,144,1076]{2,1,0:T(8,128)(2,1)} %get-tuple-element.34), channel_id=1, source_target_pairs={{0,2},{1,5},{2,0},{3,7},{4,6},{5,1},{6,4},{7,3},{8,10},{9,13},{10,... | collective-permute-start | bytes 7437320 | tf_op jit(solution)/shard_map/ppermute | solution.py:242
  318.5 59.1 %collective-permute-start.28 = (bf16[8,144,288]{2,1,0:T(8,128)(2,1)}, bf16[8,144,288]{2,1,0:T(8,128)(2,1)}, u32[]{:S(2)}, u32[]{:S(2)}) collective-permute-start(bf16[8,144,288]{2,1,0:T(8,128)(2,1)} %get-tuple-element.32), channel_id=1, source_target_pairs={{0,2},{1,5},{2,0},{3,7},{4,6},{5,1},{6,4},{7,3},{8,10},{9,13},{10,... | collective-permute-start | bytes 1990664 | tf_op jit(solution)/shard_map/ppermute | solution.py:242
  368.0 98.8 %collective-permute-start.24 = (bf16[8,144,864]{2,1,0:T(8,128)(2,1)}, bf16[8,144,864]{2,1,0:T(8,128)(2,1)}, u32[]{:S(2)}, u32[]{:S(2)}) collective-permute-start(bf16[8,144,864]{2,1,0:T(8,128)(2,1)} %get-tuple-element.30), channel_id=1, source_target_pairs={{0,2},{1,5},{2,0},{3,7},{4,6},{5,1},{6,4},{7,3},{8,10},{9,13},{10,... | collective-permute-start | bytes 5971976 | tf_op jit(solution)/shard_map/ppermute | solution.py:242
  375.2 26.5 %collective-permute-start.23 = (bf16[512,1152]{1,0:T(8,128)(2,1)}, bf16[512,1152]{1,0:T(8,128)(2,1)}, u32[]{:S(2)}, u32[]{:S(2)}) collective-permute-start(bf16[512,1152]{1,0:T(8,128)(2,1)} %slice.495), channel_id=1, source_target_pairs={{0,1},{1,0},{2,3},{3,2},{4,5},{5,4},{6,7},{7,6},{8,9},{9,8},{10,11... | collective-permute-start | bytes 3538952 | tf_op jit(solution)/shard_map/ppermute | solution.py:242
  385.0 76.4 %collective-permute-start.37 = (bf16[4,144,1076]{2,1,0:T(8,128)(2,1)}, bf16[4,144,1076]{2,1,0:T(8,128)(2,1)}, u32[]{:S(2)}, u32[]{:S(2)}) collective-permute-start(bf16[4,144,1076]{2,1,0:T(8,128)(2,1)} %get-tuple-element.71), channel_id=1, source_target_pairs={{0,4},{1,3},{2,6},{3,1},{4,0},{5,7},{6,2},{7,5},{8,12},{9,11},{10,... | collective-permute-start | bytes 3718664 | tf_op jit(solution)/shard_map/ppermute | solution.py:242
  396.0 67.1 %collective-permute-start.33 = (bf16[4,144,1076]{2,1,0:T(8,128)(2,1)}, bf16[4,144,1076]{2,1,0:T(8,128)(2,1)}, u32[]{:S(2)}, u32[]{:S(2)}) collective-permute-start(bf16[4,144,1076]{2,1,0:T(8,128)(2,1)} %get-tuple-element.73), channel_id=1, source_target_pairs={{0,4},{1,3},{2,6},{3,1},{4,0},{5,7},{6,2},{7,5},{8,12},{9,11},{10,... | collective-permute-start | bytes 3718664 | tf_op jit(solution)/shard_map/ppermute | solution.py:242
  398.9 71.9 %collective-permute-start.31 = (bf16[1,144,288]{2,1,0:T(8,128)(2,1)S(1)}, bf16[1,144,288]{2,1,0:T(8,128)(2,1)S(1)}, u32[]{:S(2)}, u32[]{:S(2)}) collective-permute-start(bf16[1,144,288]{2,1,0:T(8,128)(2,1)S(1)} %add_convert_fusion.26), channel_id=1, source_target_pairs={{0,16},{1,17},{2,18},{3,19},{4,20},{5,21},{6,22},{7,23},{8,24},{9,... | collective-permute-start | bytes 248840 | tf_op jit(solution)/shard_map/ppermute | solution.py:242
  463.0 21.5 %collective-permute-start.38 = (bf16[2,144,1076]{2,1,0:T(8,128)(2,1)S(1)}, bf16[2,144,1076]{2,1,0:T(8,128)(2,1)S(1)}, u32[]{:S(2)}, u32[]{:S(2)}) collective-permute-start(bf16[2,144,1076]{2,1,0:T(8,128)(2,1)S(1)} %get-tuple-element.87), channel_id=1, source_target_pairs={{0,8},{1,9},{2,10},{3,11},{4,12},{5,13},{6,14},{7,15},{8,0},{9,1},... | collective-permute-start | bytes 1859336 | tf_op jit(solution)/shard_map/ppermute | solution.py:242
  464.8 35.4 %collective-permute-start.34 = (bf16[2,144,1076]{2,1,0:T(8,128)(2,1)S(1)}, bf16[2,144,1076]{2,1,0:T(8,128)(2,1)S(1)}, u32[]{:S(2)}, u32[]{:S(2)}) collective-permute-start(bf16[2,144,1076]{2,1,0:T(8,128)(2,1)S(1)} %get-tuple-element.89), channel_id=1, source_target_pairs={{0,8},{1,9},{2,10},{3,11},{4,12},{5,13},{6,14},{7,15},{8,0},{9,1},... | collective-permute-start | bytes 1859336 | tf_op jit(solution)/shard_map/ppermute | solution.py:242
  468.8 31.5 %collective-permute-start.25 = (bf16[4,144,864]{2,1,0:T(8,128)(2,1)S(1)}, bf16[4,144,864]{2,1,0:T(8,128)(2,1)S(1)}, u32[]{:S(2)}, u32[]{:S(2)}) collective-permute-start(bf16[4,144,864]{2,1,0:T(8,128)(2,1)S(1)} %get-tuple-element.81), channel_id=1, source_target_pairs={{0,4},{1,3},{2,6},{3,1},{4,0},{5,7},{6,2},{7,5},{8,12},{9,11},{10,... | collective-permute-start | bytes 2985992 | tf_op jit(solution)/shard_map/ppermute | solution.py:242
  484.5 18.3 %collective-permute-start.39 = (bf16[1,144,1076]{2,1,0:T(8,128)(2,1)S(1)}, bf16[1,144,1076]{2,1,0:T(8,128)(2,1)S(1)}, u32[]{:S(2)}, u32[]{:S(2)}) collective-permute-start(bf16[1,144,1076]{2,1,0:T(8,128)(2,1)S(1)} %add_convert_fusion.18), channel_id=1, source_target_pairs={{0,16},{1,17},{2,18},{3,19},{4,20},{5,21},{6,22},{7,23},{8,24},{9,... | collective-permute-start | bytes 929672 | tf_op jit(solution)/shard_map/ppermute | solution.py:242
  500.2 19.8 %collective-permute-start.35 = (bf16[1,144,1076]{2,1,0:T(8,128)(2,1)S(1)}, bf16[1,144,1076]{2,1,0:T(8,128)(2,1)S(1)}, u32[]{:S(2)}, u32[]{:S(2)}) collective-permute-start(bf16[1,144,1076]{2,1,0:T(8,128)(2,1)S(1)} %add_convert_fusion.20), channel_id=1, source_target_pairs={{0,16},{1,17},{2,18},{3,19},{4,20},{5,21},{6,22},{7,23},{8,24},{9,... | collective-permute-start | bytes 929672 | tf_op jit(solution)/shard_map/ppermute | solution.py:242
  500.6 19.0 %collective-permute-start.26 = (bf16[2,144,864]{2,1,0:T(8,128)(2,1)S(1)}, bf16[2,144,864]{2,1,0:T(8,128)(2,1)S(1)}, u32[]{:S(2)}, u32[]{:S(2)}) collective-permute-start(bf16[2,144,864]{2,1,0:T(8,128)(2,1)S(1)} %get-tuple-element.92), channel_id=1, source_target_pairs={{0,8},{1,9},{2,10},{3,11},{4,12},{5,13},{6,14},{7,15},{8,0},{9,1},... | collective-permute-start | bytes 1493000 | tf_op jit(solution)/shard_map/ppermute | solution.py:242
  (68 other events, 717.1 us)
